TPU v7x, 32 devices: a whole 2x2x4 slice. The times are simulated.
32 devices in a mesh: bxy: 8 (over z, x), bz: 4 (over y, core).
Axes of the slice: x: 2, y: 2, z: 4, core: 2. Of those that a mesh axis runs over, the one named last changes fastest.
Arguments:
- basis: float32 [48, 245760], P(None, ('bxy', 'bz')), may hold values from -12 to 12
- velocity: float32 [3, 8, 48, 128], P(None, 'bxy'), may hold values from -0.2 to 0.2
- temper: float32 [8, 48, 128], P('bxy'), may hold values from 0.5 to 1.5
- flags: int32 [8, 48, 128], P('bxy'), may hold values 0 or 1
- order: int32 [8, 30720], P('bxy'), may hold values from 0 to 30719, each once within a row
Outputs:
- ortho: float32 [16, 245760], P(None, ('bxy', 'bz'))
- proj: float32 [48, 16], replicated
- upper: float32 [16, 16], replicated
Inputs may be any that keep to these rules, and one draw needn't show every extreme that they name: `order`: for each slab, a permutation of its 30720 local rows.
All inputs are finite; a program needn't handle non-finite values. No bound on the sum of `flags` on one device may be relied on, other than what follows from the above.
Results may differ from a plain program's by a relative error of at most 0.0003.
Values sent between devices are 32-bit elements; how exact they have to be, the bound alone decides.
A program may use at most 128 MiB of HBM per device.

v0:
```python
import jax
import jax.numpy as jnp
from jax import lax
from jax.sharding import PartitionSpec as P

BLK = 16
KB = 48
STEPS = 2


FLOW_DIRS = (
    (0, 0, 0),
    (1, 0, 0),
    (-1, 0, 0),
    (0, 1, 0),
    (0, -1, 0),
    (0, 0, 1),
    (0, 0, -1),
    (1, 1, 0),
    (-1, -1, 0),
    (1, -1, 0),
    (-1, 1, 0),
    (1, 0, 1),
    (-1, 0, -1),
    (1, 0, -1),
    (-1, 0, 1),
    (0, 1, 1),
    (0, -1, -1),
    (0, 1, -1),
    (0, -1, 1),
)
ALL_DIRS = FLOW_DIRS + FLOW_DIRS[:7]
FLOW_WEIGHTS = (1.0 / 3.0,) + (1.0 / 18.0,) * 6 + (1.0 / 36.0,) * 12
HEAT_WEIGHTS = (0.25,) + (0.125,) * 6
OPPOSITE = (0,) + tuple((number + 1 if number % 2 == 1 else number - 1 for number in range(1, 19)))
OMEGA_FLOW = 1.6
OMEGA_HEAT = 1.4
BUOYANCY = 0.2


def with_halo(block, sides, width):
    for axis, dim in sides:
        count = lax.axis_size(axis)
        forward = [(i, i + 1) for i in range(count - 1)]
        forward.append((count - 1, 0))
        backward = [(target, source) for source, target in forward]
        low = lax.ppermute(
            lax.slice_in_dim(block, block.shape[dim] - width, None, axis=dim), axis, forward
        )
        high = lax.ppermute(lax.slice_in_dim(block, 0, width, axis=dim), axis, backward)
        block = jnp.concatenate([low, block, high], axis=dim)
    return block


def along(direction, comps):
    total = 0.0
    for weight, array in zip(direction, comps):
        if weight == 1:
            total = total + array
        elif weight == -1:
            total = total - array
    return total


def moments(flow, heat):
    density = flow[0]
    for number in range(1, 19):
        density = density + flow[number]
    momentum = []
    for comp in range(3):
        momentum.append(along([FLOW_DIRS[number][comp] for number in range(19)], flow))
    warmth = heat[0]
    for number in range(1, 7):
        warmth = warmth + heat[number]
    return (density, momentum, warmth)


def equilibria(density, momentum, warmth, velocity, temper):
    carried = [momentum[comp] - velocity[comp] * density for comp in range(3)]
    speed_sq = velocity[0] * velocity[0] + velocity[1] * velocity[1] + velocity[2] * velocity[2]
    carried_u = velocity[0] * carried[0] + velocity[1] * carried[1] + velocity[2] * carried[2]
    flow_eq = []
    heat_eq = []
    for number in range(19):
        drift = along(FLOW_DIRS[number], velocity)
        push = along(FLOW_DIRS[number], carried)
        value = (
            density * (1.0 + 3.0 * drift + 4.5 * drift * drift - 1.5 * speed_sq)
            + 3.0 * push
            + 9.0 * drift * push
            - 3.0 * carried_u
        )
        flow_eq.append(FLOW_WEIGHTS[number] * value)
        if number < 7:
            heat_eq.append(
                HEAT_WEIGHTS[number] * (warmth * (1.0 + 4.0 * drift) + 4.0 * temper * push)
            )
    return (flow_eq, heat_eq)


def collide(flow, heat, velocity, temper, solid):
    density, momentum, warmth = moments(flow, heat)
    flow_eq, heat_eq = equilibria(density, momentum, warmth, velocity, temper)
    flow_new = []
    heat_new = []
    for number in range(19):
        fresh = (
            flow[number]
            - OMEGA_FLOW * (flow[number] - flow_eq[number])
            + 3.0 * FLOW_WEIGHTS[number] * FLOW_DIRS[number][1] * BUOYANCY * warmth
        )
        flow_new.append(jnp.where(solid, flow[OPPOSITE[number]], fresh))
    for number in range(7):
        fresh = heat[number] - OMEGA_HEAT * (heat[number] - heat_eq[number])
        heat_new.append(jnp.where(solid, heat[OPPOSITE[number]], fresh))
    return (flow_new, heat_new)


def stream(flow, heat):
    stacked = jnp.stack(flow + heat, 1)
    cells_first = stacked.shape[2]
    padded = with_halo(stacked, (("bxy", 2),), 1)
    moved = []
    for number in range(26):
        first, second, third = ALL_DIRS[number]
        piece = padded[:, number, 1 - first : 1 - first + cells_first]
        moved.append(jnp.roll(piece, (second, third), axis=(2, 3)))
    return (moved[:19], moved[19:])


def body(basis, velocity, temper, flags, order):
    count_first = lax.axis_size("bxy")
    count_second = lax.axis_size("bz")
    devices = count_first * count_second
    panel_rows = basis.shape[1]
    piece_rows = panel_rows // count_first
    slab_rows = piece_rows * devices
    total_rows = panel_rows * devices
    vectors = BLK // count_second
    cells_first, cells_vertical, cells_third = temper.shape
    permute = order.reshape(slab_rows)
    block = basis[KB - BLK :]
    outgoing = (
        block.reshape(count_second, vectors, count_first, piece_rows)
        .transpose(2, 0, 1, 3)
        .reshape(count_first, count_second, vectors * piece_rows)
    )
    arrived = lax.all_to_all(
        lax.all_to_all(outgoing, "bxy", split_axis=0, concat_axis=0, tiled=True),
        "bz",
        split_axis=1,
        concat_axis=1,
        tiled=True,
    )
    permuted = (
        arrived.reshape(devices, vectors, piece_rows).transpose(1, 0, 2).reshape(vectors, slab_rows)
    )
    inverse = jnp.zeros((slab_rows,), jnp.int32).at[permute].set(lax.iota(jnp.int32, slab_rows))
    fields = jnp.take(permuted, inverse, axis=1).reshape(
        vectors, 5, cells_first, cells_vertical, cells_third
    )
    height = lax.broadcasted_iota(jnp.int32, temper.shape, 1)
    solid = (flags == 1) | (height == 0) | (height == cells_vertical - 1)
    speeds = [velocity[0], velocity[1], velocity[2]]
    flow, heat = equilibria(
        fields[:, 0], [fields[:, 1], fields[:, 2], fields[:, 3]], fields[:, 4], speeds, temper
    )
    for turn in range(STEPS):
        flow, heat = collide(flow, heat, speeds, temper, solid)
        flow, heat = stream(flow, heat)
    density, momentum, warmth = moments(flow, heat)
    evolved = jnp.stack([density] + momentum + [warmth], 1).reshape(vectors, slab_rows)
    reordered = jnp.take(evolved, permute, axis=1)
    leaving = (
        reordered.reshape(vectors, devices, piece_rows)
        .transpose(1, 0, 2)
        .reshape(count_first, count_second, vectors * piece_rows)
    )
    landed = lax.all_to_all(
        lax.all_to_all(leaving, "bxy", split_axis=0, concat_axis=0, tiled=True),
        "bz",
        split_axis=1,
        concat_axis=1,
        tiled=True,
    )
    work = (
        landed.reshape(count_first, count_second, vectors, piece_rows)
        .transpose(1, 2, 0, 3)
        .reshape(BLK, panel_rows)
    )
    highest = lax.Precision.HIGHEST
    proj = lax.psum(jnp.dot(basis, work.T, precision=highest), ("bxy", "bz")) / total_rows
    resid = work - jnp.dot(proj.T, basis, precision=highest)
    gram = lax.psum(jnp.dot(resid, resid.T, precision=highest), ("bxy", "bz")) / total_rows
    lower = jnp.linalg.cholesky(gram)
    ortho = lax.linalg.triangular_solve(lower, resid, left_side=True, lower=True)
    return (ortho, proj, lower.T)


def solution(mesh):
    in_specs = (
        P(None, ("bxy", "bz")),
        P(None, "bxy", None, None),
        P("bxy", None, None),
        P("bxy", None, None),
        P("bxy", None),
    )
    out_specs = (P(None, ("bxy", "bz")), P(), P())
    return jax.shard_map(body, mesh=mesh, in_specs=in_specs, out_specs=out_specs, check_vma=False)
```

profile of v0, /device:TPU:0, one launch (start us, length us, event | category | flops | bytes accessed | tf_op | source)
XLA Modules:
  0.0 866.8 jit_solution(10909693451114125009)
XLA Ops:
  0.6 1.1 slice.421
  2.8 1.0 copy.2515
  3.8 7.4 all-to-all-start
  13.4 112.7 %scatter_custom_fusion = s32[30720]{0:T(1024)S(1)} fusion(s32[30720]{0:T(1024)S(1)} %bitcast.831, s32[30720]{0:T(1024)S(1)} %iota.42, s32[]{:T(128)} %constant.78.clone.1), kind=kCustom, calls=%fused_computation.506 | custom fusion | bytes 122884 | tf_op jit(solution)/shard_map/scatter | solution.py:158
  128.2 0.9 copy.2516
  129.1 3.6 all-to-all-start.1
  132.8 0.8 multiply_bitcast_fusion.2
  133.6 7.5 all-to-all-done.1
  141.9 8.0 copy.2518
  150.0 107.6 %gather_fusion = f32[30720,4]{1,0:T(8,128)} fusion(f32[4,30720]{0,1:T(8,128)} %bitcast.781, s32[30720]{0:T(1024)S(1)} %get-tuple-element.358), kind=kCustom, calls=%fused_computation.clone | custom fusion | bytes 1105920 | tf_op jit(solution)/shard_map/jit(_take)/gather | solution.py:159
  257.6 18.2 %broadcast_select_fusion.1 = f32[30720,4]{1,0:T(8,128)} fusion(f32[30720,4]{1,0:T(8,128)} %gather_fusion, pred[30720]{0:T(1024)(128)(4,1)S(1)} %compare_and_fusion.1), kind=kLoop, calls=%fused_computation.5 | loop fusion | flops 122880 | bytes 1013760 | tf_op jit(solution)/shard_map/jit(_take)/select_n | solution.py:159
  275.8 11.4 %fusion.212 = (f32[4,1,1,48,128]{0,4,3,1,2:T(8,128)}, f32[4,1,1,48,128]{0,4,3,1,2:T(8,128)}, f32[4,1,1,48,128]{0,4,3,1,2:T(8,128)}, f32[4,1,1,48,128]{0,4,3,1,2:T(8,128)S(1)}, f32[4,1,1,48,128]{0,4,3,1,2:T(8,128)}) fusion(f32[4,5,1,48,128]{0,4,3,1,2:T(8,128)} %bitcast.778), kind=kLoop, calls=%fused_computation.671 | loop fusion | bytes 983040 | tf_op jit(solution)/shard_map/slice | solution.py:166
  287.2 1.2 copy.2717
  288.3 1.8 copy.2521
  290.1 2.4 copy.2721
  292.5 2.5 copy.2718
  295.0 3.0 copy.2719
  298.0 1.8 copy.2720
  300.2 1.1 add_multiply_fusion.12
  301.3 0.9 fusion.139
  302.2 3.1 subtract_select_fusion.14
  305.7 2.7 subtract_select_fusion.15
  308.7 1.0 subtract_select_fusion.19
  329.2 4.7 collective-permute-start.1
  334.9 0.8 add_select_fusion.32
  342.9 0.8 fusion.225
  344.0 0.8 copy.2603
  344.9 0.8 copy.2600
  345.7 0.8 copy.2564
  347.5 0.8 copy.2585
  348.3 0.8 copy.2587
  353.6 0.8 slice_bitcast_fusion.44
  355.2 0.8 slice_bitcast_fusion.50
  356.0 85.6 %collective-permute-done.1 = f32[4,26,1,48,128]{4,3,2,1,0:T(8,128)} collective-permute-done((f32[4,26,1,48,128]{4,3,2,1,0:T(8,128)}, f32[4,26,1,48,128]{4,3,2,1,0:T(8,128)}, u32[]{:S(2)}, u32[]{:S(2)}) %collective-permute-start.1) | collective-permute-done | bytes 2555936 | tf_op jit(solution)/shard_map/ppermute | solution.py:50
  441.6 1.2 fusion.216
  444.0 1.2 fusion.215
  452.4 0.8 copy.2573
  455.0 0.8 copy.2582
  455.9 2.8 subtract_select_fusion.5
  458.9 1.2 subtract_select_fusion.7
  481.2 4.9 collective-permute-start.3
  486.3 2.0 subtract_select_fusion.4
  497.3 93.8 %collective-permute-done.2 = f32[4,26,1,48,128]{4,3,2,1,0:T(8,128)} collective-permute-done((f32[4,26,1,48,128]{4,3,2,1,0:T(8,128)}, f32[4,26,1,48,128]{4,3,2,1,0:T(8,128)}, u32[]{:S(2)}, u32[]{:S(2)}) %collective-permute-start.2) | collective-permute-done | bytes 2555936 | tf_op jit(solution)/shard_map/ppermute | solution.py:47
  591.2 1.9 fusion.213
  593.8 1.9 fusion.214
  597.8 0.8 copy.2659
  599.5 0.8 copy.2663
  600.4 0.8 copy.2667
  601.2 1.7 subtract_add_fusion
  603.2 1.2 fusion.20
  604.4 1.1 constant_dynamic-update-slice_fusion.56
  605.9 7.7 copy.2716
  613.6 107.6 %gather_fusion.1 = f32[30720,4]{1,0:T(8,128)} fusion(f32[4,30720]{0,1:T(8,128)} %bitcast.780, s32[30720]{0:T(1024)S(1)} %copy-done.119), kind=kCustom, calls=%fused_computation.1.clone | custom fusion | bytes 1105920 | tf_op jit(solution)/shard_map/jit(_take)/gather | solution.py:173
  721.3 18.2 %broadcast_select_fusion = f32[30720,4]{1,0:T(8,128)} fusion(f32[30720,4]{1,0:T(8,128)} %gather_fusion.1, pred[30720]{0:T(1024)(128)(4,1)S(1)} %copy-done.140), kind=kLoop, calls=%fused_computation.4 | loop fusion | flops 122880 | bytes 1013760 | tf_op jit(solution)/shard_map/jit(_take)/select_n | solution.py:173
  739.4 9.0 %copy.2703 = f32[4,32,960]{2,0,1:T(4,128)S(1)} copy(f32[4,32,960]{0,2,1:T(8,128)} %bitcast.779) | data formatting | bytes 983040 | tf_op jit(solution)/shard_map/reshape | solution.py:175
  749.1 17.0 %all_to_all.20 = f32[8,4,3840]{2,1,0:T(4,128)S(1)} all-to-all(f32[8,4,3840]{2,1,0:T(4,128)S(1)} %reshape.26161), channel_id=1, replica_groups=mesh['bxy'=8,'bz'=4] {'bxy'}, dimensions={0} | all-to-all | bytes 983040 | tf_op jit(solution)/shard_map/all_to_all | solution.py:180
  766.2 11.2 %all_to_all.21 = f32[8,4,3840]{2,0,1:T(8,128)S(1)} all-to-all(f32[8,4,3840]{2,0,1:T(8,128)S(1)} %copy.2704), channel_id=1, replica_groups=mesh['bxy'=8,'bz'=4] {'bz'}, dimensions={1} | all-to-all | bytes 983040 | tf_op jit(solution)/shard_map/all_to_all | solution.py:179
  778.4 1.2 convolution_bitcast_fusion
  779.6 38.9 %psum.14 = f32[48,16]{0,1:T(8,128)S(1)} all-reduce(f32[48,16]{0,1:T(8,128)S(1)} %convolution_bitcast_fusion), channel_id=1, replica_groups=mesh['bxy'=8,'bz'=4] {'bxy','bz'}, use_global_device_ids=true, to_apply=%region_1.0 | all-reduce | flops 768 | bytes 6144 | tf_op jit(solution)/shard_map/psum | solution.py:192
  818.5 0.8 convolution_subtract_fusion
  820.1 40.4 %psum.15 = f32[16,16]{0,1:T(8,128)S(1)} all-reduce(f32[16,16]{0,1:T(8,128)S(1)} %fusion.217), channel_id=1, replica_groups=mesh['bxy'=8,'bz'=4] {'bxy','bz'}, use_global_device_ids=true, to_apply=%region_2.4 | all-reduce | flops 256 | bytes 2048 | tf_op jit(solution)/shard_map/psum | solution.py:194
  860.6 1.5 cholesky.16
  863.4 1.2 custom-call.6
  864.6 1.4 fusion.196
  (578 shorter events, 88.8 us)
Async XLA Ops:
  1.7 9.5 %copy-start.61 = (f32[3,1,48,128]{3,2,1,0:T(8,128)S(1)}, f32[3,1,48,128]{3,2,1,0:T(8,128)}, u32[]{:S(2)}) copy-start(f32[3,1,48,128]{3,2,1,0:T(8,128)} %param.8) | copy-start | bytes 221188
  2.0 10.7 %copy-start.150 = (f32[1,48,128]{2,1,0:T(8,128)S(1)}, f32[1,48,128]{2,1,0:T(8,128)}, u32[]{:S(2)}) copy-start(f32[1,48,128]{2,1,0:T(8,128)} %param.9) | copy-start | bytes 73732
  2.0 11.3 %copy-start.62 = (s32[1,30720]{1,0:T(1,128)S(1)}, s32[1,30720]{1,0:T(1,128)}, u32[]{:S(2)}) copy-start(s32[1,30720]{1,0:T(1,128)} %param.11) | copy-start | bytes 368644
  3.8 128.9 %copy-start.151 = (s32[1,48,128]{2,1,0:T(8,128)S(1)}, s32[1,48,128]{2,1,0:T(8,128)}, u32[]{:S(2)}) copy-start(s32[1,48,128]{2,1,0:T(8,128)} %param.10) | copy-start | bytes 73732
  3.8 124.4 %all-to-all-start = ((f32[8,4,3840]{2,1,0:T(4,128)}), f32[8,4,3840]{2,1,0:T(4,128)S(1)}, u32[]{:S(2)}, u32[]{:S(2)}) async-start(f32[8,4,3840]{2,1,0:T(4,128)} %copy.2515), calls=%async_computation | async-start | bytes 983040 | tf_op jit(solution)/shard_map/all_to_all | solution.py:149
  129.1 12.1 %all-to-all-start.1 = ((f32[8,4,3840]{2,0,1:T(8,128)}), f32[8,4,3840]{2,0,1:T(8,128)S(1)}, u32[]{:S(2)}, u32[]{:S(2)}) async-start(f32[8,4,3840]{2,0,1:T(8,128)} %copy.2516), calls=%async_computation.1 | async-start | bytes 983040 | tf_op jit(solution)/shard_map/all_to_all | solution.py:148
  299.8 5.6 copy-start.13
  299.8 5.6 copy-start.15
  299.8 5.6 copy-start.17
  299.8 5.6 copy-start.19
  299.9 5.6 copy-start.21
  299.9 5.6 copy-start.23
  299.9 5.6 copy-start.25
  299.9 5.6 copy-start.27
  299.9 5.6 copy-start.29
  299.9 5.6 copy-start.31
  305.3 33.9 %copy-start.120 = (f32[4,1,48,128]{3,0,2,1:T(4,128)}, f32[4,1,48,128]{3,0,2,1:T(4,128)S(1)}, u32[]{:S(2)}) copy-start(f32[4,1,48,128]{3,0,2,1:T(4,128)S(1)} %get-tuple-element.78) | copy-start | bytes 294916
  329.2 112.4 %collective-permute-start.1 = (f32[4,26,1,48,128]{4,3,2,1,0:T(8,128)}, f32[4,26,1,48,128]{4,3,2,1,0:T(8,128)}, u32[]{:S(2)}, u32[]{:S(2)}) collective-permute-start(f32[4,26,1,48,128]{4,3,2,1,0:T(8,128)} %constant_dynamic-update-slice_fusion), channel_id=1, source_target_pairs={{4,0},{8,4},{12,8},{16,12},{20,16},{24,20},{28,24},{0,28},{5,1},{9... | collective-permute-start | bytes 7667720 | tf_op jit(solution)/shard_map/ppermute | solution.py:50
  333.9 110.1 %collective-permute-start = (f32[4,26,1,48,128]{4,3,2,1,0:T(8,128)}, f32[4,26,1,48,128]{4,3,2,1,0:T(8,128)}, u32[]{:S(2)}, u32[]{:S(2)}) collective-permute-start(f32[4,26,1,48,128]{4,3,2,1,0:T(8,128)} %constant_dynamic-update-slice_fusion), channel_id=1, source_target_pairs={{0,4},{4,8},{8,12},{12,16},{16,20},{20,24},{24,28},{28,0},{1,5},{5... | collective-permute-start | bytes 7667720 | tf_op jit(solution)/shard_map/ppermute | solution.py:47
  337.0 11.4 %copy-start.97 = (f32[4,1,48,1]{3,0,2,1:T(4,128)}, f32[4,1,48,1]{3,0,2,1:T(4,128)S(1)}, u32[]{:S(2)}) copy-start(f32[4,1,48,1]{3,0,2,1:T(4,128)S(1)} %slice_maximum_fusion.5) | copy-start | bytes 2308
  337.0 13.0 %copy-start.99 = (f32[4,1,48,1]{3,0,2,1:T(4,128)}, f32[4,1,48,1]{3,0,2,1:T(4,128)S(1)}, u32[]{:S(2)}) copy-start(f32[4,1,48,1]{3,0,2,1:T(4,128)S(1)} %pad_maximum_fusion.6) | copy-start | bytes 2308
  338.6 11.4 %copy-start.101 = (f32[4,1,48,1]{3,0,2,1:T(4,128)}, f32[4,1,48,1]{3,0,2,1:T(4,128)S(1)}, u32[]{:S(2)}) copy-start(f32[4,1,48,1]{3,0,2,1:T(4,128)S(1)} %slice_maximum_fusion.2) | copy-start | bytes 2308
  339.9 11.6 %copy-start.121 = (f32[4,1,48,128]{3,0,2,1:T(4,128)S(1)}, f32[4,1,48,128]{3,0,2,1:T(4,128)}, u32[]{:S(2)}) copy-start(f32[4,1,48,128]{3,0,2,1:T(4,128)} %copy-done.120) | copy-start | bytes 294916
  340.5 10.3 %copy-start.103 = (f32[4,1,48,1]{3,0,2,1:T(4,128)}, f32[4,1,48,1]{3,0,2,1:T(4,128)S(1)}, u32[]{:S(2)}) copy-start(f32[4,1,48,1]{3,0,2,1:T(4,128)S(1)} %pad_maximum_fusion.5) | copy-start | bytes 2308
  343.8 7.7 copy-start.105
  343.9 98.9 %copy-start.107 = (f32[4,1,48,1]{3,0,2,1:T(4,128)}, f32[4,1,48,1]{3,0,2,1:T(4,128)S(1)}, u32[]{:S(2)}) copy-start(f32[4,1,48,1]{3,0,2,1:T(4,128)S(1)} %slice.565) | copy-start | bytes 2308
  351.5 107.3 %copy-start.6 = (f32[4,1,1,47,128]{4,0,3,2,1:T(4,128)}, f32[4,1,1,47,128]{4,0,3,2,1:T(4,128)S(1)}, u32[]{:S(2)}) copy-start(f32[4,1,1,47,128]{4,0,3,2,1:T(4,128)S(1)} %get-tuple-element.289) | copy-start | bytes 288772
  352.2 106.6 %copy-start.8 = (f32[4,1,1,47,128]{4,0,3,2,1:T(4,128)}, f32[4,1,1,47,128]{4,0,3,2,1:T(4,128)S(1)}, u32[]{:S(2)}) copy-start(f32[4,1,1,47,128]{4,0,3,2,1:T(4,128)S(1)} %get-tuple-element.287) | copy-start | bytes 288772
  352.2 103.6 %copy-start.10 = (f32[4,1,1,47,128]{4,0,3,2,1:T(4,128)}, f32[4,1,1,47,128]{4,0,3,2,1:T(4,128)S(1)}, u32[]{:S(2)}) copy-start(f32[4,1,1,47,128]{4,0,3,2,1:T(4,128)S(1)} %get-tuple-element.265) | copy-start | bytes 288772
  464.3 21.8 %copy-start.98 = (f32[4,1,48,1]{3,0,2,1:T(4,128)S(1)}, f32[4,1,48,1]{3,0,2,1:T(4,128)}, u32[]{:S(2)}) copy-start(f32[4,1,48,1]{3,0,2,1:T(4,128)} %copy-done.97) | copy-start | bytes 2308
  464.3 21.8 %copy-start.100 = (f32[4,1,48,1]{3,0,2,1:T(4,128)S(1)}, f32[4,1,48,1]{3,0,2,1:T(4,128)}, u32[]{:S(2)}) copy-start(f32[4,1,48,1]{3,0,2,1:T(4,128)} %copy-done.99) | copy-start | bytes 2308
  464.3 21.8 %copy-start.102 = (f32[4,1,48,1]{3,0,2,1:T(4,128)S(1)}, f32[4,1,48,1]{3,0,2,1:T(4,128)}, u32[]{:S(2)}) copy-start(f32[4,1,48,1]{3,0,2,1:T(4,128)} %copy-done.101) | copy-start | bytes 2308
  464.3 21.8 %copy-start.104 = (f32[4,1,48,1]{3,0,2,1:T(4,128)S(1)}, f32[4,1,48,1]{3,0,2,1:T(4,128)}, u32[]{:S(2)}) copy-start(f32[4,1,48,1]{3,0,2,1:T(4,128)} %copy-done.103) | copy-start | bytes 2308
  464.3 21.8 %copy-start.106 = (f32[4,1,48,1]{3,0,2,1:T(4,128)S(1)}, f32[4,1,48,1]{3,0,2,1:T(4,128)}, u32[]{:S(2)}) copy-start(f32[4,1,48,1]{3,0,2,1:T(4,128)} %copy-done.105) | copy-start | bytes 2308
  464.3 21.8 %copy-start.108 = (f32[4,1,48,1]{3,0,2,1:T(4,128)S(1)}, f32[4,1,48,1]{3,0,2,1:T(4,128)}, u32[]{:S(2)}) copy-start(f32[4,1,48,1]{3,0,2,1:T(4,128)} %copy-done.107) | copy-start | bytes 2308
  464.3 21.8 %copy-start.113 = (f32[4,1,47,128]{3,0,2,1:T(4,128)S(1)}, f32[4,1,47,128]{3,0,2,1:T(4,128)}, u32[]{:S(2)}) copy-start(f32[4,1,47,128]{3,0,2,1:T(4,128)} %get-tuple-element.290) | copy-start | bytes 288772
  464.4 21.8 %copy-start.114 = (f32[4,1,47,128]{3,0,2,1:T(4,128)S(1)}, f32[4,1,47,128]{3,0,2,1:T(4,128)}, u32[]{:S(2)}) copy-start(f32[4,1,47,128]{3,0,2,1:T(4,128)} %get-tuple-element.288) | copy-start | bytes 288772
  464.4 21.8 %copy-start.115 = (f32[4,1,47,128]{3,0,2,1:T(4,128)S(1)}, f32[4,1,47,128]{3,0,2,1:T(4,128)}, u32[]{:S(2)}) copy-start(f32[4,1,47,128]{3,0,2,1:T(4,128)} %get-tuple-element.284) | copy-start | bytes 288772
  464.4 21.8 %copy-start.116 = (f32[4,1,47,128]{3,0,2,1:T(4,128)S(1)}, f32[4,1,47,128]{3,0,2,1:T(4,128)}, u32[]{:S(2)}) copy-start(f32[4,1,47,128]{3,0,2,1:T(4,128)} %get-tuple-element.278) | copy-start | bytes 288772
  464.4 21.8 %copy-start.117 = (f32[4,1,47,128]{3,0,2,1:T(4,128)S(1)}, f32[4,1,47,128]{3,0,2,1:T(4,128)}, u32[]{:S(2)}) copy-start(f32[4,1,47,128]{3,0,2,1:T(4,128)} %get-tuple-element.274) | copy-start | bytes 288772
  464.4 21.8 %copy-start.118 = (f32[4,1,47,128]{3,0,2,1:T(4,128)S(1)}, f32[4,1,47,128]{3,0,2,1:T(4,128)}, u32[]{:S(2)}) copy-start(f32[4,1,47,128]{3,0,2,1:T(4,128)} %get-tuple-element.272) | copy-start | bytes 288772
  464.4 21.8 %copy-start.130 = (f32[4,1,48,127]{3,0,2,1:T(4,128)S(1)}, f32[4,1,48,127]{3,0,2,1:T(4,128)}, u32[]{:S(2)}) copy-start(f32[4,1,48,127]{3,0,2,1:T(4,128)} %slice_maximum_fusion.4) | copy-start | bytes 292612
  464.4 21.8 %copy-start.131 = (f32[4,1,48,127]{3,0,2,1:T(4,128)S(1)}, f32[4,1,48,127]{3,0,2,1:T(4,128)}, u32[]{:S(2)}) copy-start(f32[4,1,48,127]{3,0,2,1:T(4,128)} %slice_maximum_fusion.3) | copy-start | bytes 292612
  464.4 21.8 %copy-start.132 = (f32[4,1,48,127]{3,0,2,1:T(4,128)S(1)}, f32[4,1,48,127]{3,0,2,1:T(4,128)}, u32[]{:S(2)}) copy-start(f32[4,1,48,127]{3,0,2,1:T(4,128)} %get-tuple-element.248) | copy-start | bytes 292612
  464.4 21.8 %copy-start.133 = (f32[4,1,48,127]{3,0,2,1:T(4,128)S(1)}, f32[4,1,48,127]{3,0,2,1:T(4,128)}, u32[]{:S(2)}) copy-start(f32[4,1,48,127]{3,0,2,1:T(4,128)} %get-tuple-element.246) | copy-start | bytes 292612
  464.4 21.8 %copy-start.134 = (f32[4,1,48,127]{3,0,2,1:T(4,128)S(1)}, f32[4,1,48,127]{3,0,2,1:T(4,128)}, u32[]{:S(2)}) copy-start(f32[4,1,48,127]{3,0,2,1:T(4,128)} %get-tuple-element.294) | copy-start | bytes 292612
  464.5 21.8 %copy-start.135 = (f32[4,1,48,127]{3,0,2,1:T(4,128)S(1)}, f32[4,1,48,127]{3,0,2,1:T(4,128)}, u32[]{:S(2)}) copy-start(f32[4,1,48,127]{3,0,2,1:T(4,128)} %get-tuple-element.296) | copy-start | bytes 292612
  464.5 21.8 %copy-start.136 = (f32[4,1,48,127]{3,0,2,1:T(4,128)S(1)}, f32[4,1,48,127]{3,0,2,1:T(4,128)}, u32[]{:S(2)}) copy-start(f32[4,1,48,127]{3,0,2,1:T(4,128)} %get-tuple-element.260) | copy-start | bytes 292612
  464.5 21.8 %copy-start.137 = (f32[4,1,48,127]{3,0,2,1:T(4,128)S(1)}, f32[4,1,48,127]{3,0,2,1:T(4,128)}, u32[]{:S(2)}) copy-start(f32[4,1,48,127]{3,0,2,1:T(4,128)} %get-tuple-element.258) | copy-start | bytes 292612
  464.5 21.8 %copy-start.148 = (f32[4,1,1,128]{3,0,2,1:T(4,128)S(1)}, f32[4,1,1,128]{3,0,2,1:T(4,128)}, u32[]{:S(2)}) copy-start(f32[4,1,1,128]{3,0,2,1:T(4,128)} %get-tuple-element.268) | copy-start | bytes 6148
  464.5 21.8 %copy-start.149 = (f32[4,1,1,128]{3,0,2,1:T(4,128)S(1)}, f32[4,1,1,128]{3,0,2,1:T(4,128)}, u32[]{:S(2)}) copy-start(f32[4,1,1,128]{3,0,2,1:T(4,128)} %get-tuple-element.262) | copy-start | bytes 6148
  464.5 21.8 %copy-start.152 = (f32[4,1,1,128]{3,0,2,1:T(4,128)S(1)}, f32[4,1,1,128]{3,0,2,1:T(4,128)}, u32[]{:S(2)}) copy-start(f32[4,1,1,128]{3,0,2,1:T(4,128)} %get-tuple-element.292) | copy-start | bytes 6148
  464.5 21.8 %copy-start.153 = (f32[4,1,1,128]{3,0,2,1:T(4,128)S(1)}, f32[4,1,1,128]{3,0,2,1:T(4,128)}, u32[]{:S(2)}) copy-start(f32[4,1,1,128]{3,0,2,1:T(4,128)} %get-tuple-element.286) | copy-start | bytes 6148
  464.5 21.8 %copy-start.154 = (f32[4,1,1,128]{3,0,2,1:T(4,128)S(1)}, f32[4,1,1,128]{3,0,2,1:T(4,128)}, u32[]{:S(2)}) copy-start(f32[4,1,1,128]{3,0,2,1:T(4,128)} %get-tuple-element.282) | copy-start | bytes 6148
  464.5 21.8 %copy-start.155 = (f32[4,1,1,128]{3,0,2,1:T(4,128)S(1)}, f32[4,1,1,128]{3,0,2,1:T(4,128)}, u32[]{:S(2)}) copy-start(f32[4,1,1,128]{3,0,2,1:T(4,128)} %get-tuple-element.280) | copy-start | bytes 6148
  464.5 21.8 %copy-start.156 = (f32[4,1,1,128]{3,0,2,1:T(4,128)S(1)}, f32[4,1,1,128]{3,0,2,1:T(4,128)}, u32[]{:S(2)}) copy-start(f32[4,1,1,128]{3,0,2,1:T(4,128)} %get-tuple-element.276) | copy-start | bytes 6148
  464.6 21.8 %copy-start.157 = (f32[4,1,1,128]{3,0,2,1:T(4,128)S(1)}, f32[4,1,1,128]{3,0,2,1:T(4,128)}, u32[]{:S(2)}) copy-start(f32[4,1,1,128]{3,0,2,1:T(4,128)} %get-tuple-element.270) | copy-start | bytes 6148
  481.0 110.2 %collective-permute-start.2 = (f32[4,26,1,48,128]{4,3,2,1,0:T(8,128)}, f32[4,26,1,48,128]{4,3,2,1,0:T(8,128)}, u32[]{:S(2)}, u32[]{:S(2)}) collective-permute-start(f32[4,26,1,48,128]{4,3,2,1,0:T(8,128)} %constant_dynamic-update-slice_fusion.26), channel_id=1, source_target_pairs={{0,4},{4,8},{8,12},{12,16},{16,20},{20,24},{24,28},{28,0},{1,5},{5... | collective-permute-start | bytes 7667720 | tf_op jit(solution)/shard_map/ppermute | solution.py:47
  481.2 112.6 %collective-permute-start.3 = (f32[4,26,1,48,128]{4,3,2,1,0:T(8,128)}, f32[4,26,1,48,128]{4,3,2,1,0:T(8,128)}, u32[]{:S(2)}, u32[]{:S(2)}) collective-permute-start(f32[4,26,1,48,128]{4,3,2,1,0:T(8,128)} %constant_dynamic-update-slice_fusion.26), channel_id=1, source_target_pairs={{4,0},{8,4},{12,8},{16,12},{20,16},{24,20},{28,24},{0,28},{5,1},{9... | collective-permute-start | bytes 7667720 | tf_op jit(solution)/shard_map/ppermute | solution.py:50
  593.2 8.0 copy-start.122
  605.9 7.8 copy-start.119
  613.6 107.6 %copy-start.140 = (pred[30720]{0:T(1024)(128)(4,1)S(1)}, pred[30720]{0:T(1024)(128)(4,1)}, u32[]{:S(2)}) copy-start(pred[30720]{0:T(1024)(128)(4,1)} %compare_and_fusion) | copy-start | bytes 92164
  766.1 12.3 %copy-start.1 = (f32[48,7680]{1,0:T(8,128)S(1)}, f32[48,7680]{1,0:T(8,128)}, u32[]{:S(2)}) copy-start(f32[48,7680]{1,0:T(8,128)} %param.7) | copy-start | bytes 4423684
  818.5 48.1 %copy-start.147 = (f32[48,16]{0,1:T(8,128)}, f32[48,16]{0,1:T(8,128)S(1)}, u32[]{:S(2)}) copy-start(f32[48,16]{0,1:T(8,128)S(1)} %broadcast_multiply_fusion.3) | copy-start | bytes 9220
  (100 other events, 313.1 us)
where the time goes:
time: 871 us; the launch traced here: 867 us
  local copies, waits for them, and re-layouts  462 us (53%)
  waiting for transfers between devices  188 us (22%)
  blocking collectives  107 us (12%)
  other arithmetic  80.7 us (9%)
  starting transfers between devices  21.1 us (2%)
    scatter x1, local copies, waits for them, and re-layouts, body(): jnp.zeros((slab_rows,), jnp.int32).at[permute]  113 us
    gather x1, local copies, waits for them, and re-layouts, body(): reordered = jnp.take(evolved, permute, axis=1)  108 us
    gather x1, local copies, waits for them, and re-layouts, body(): jnp.take(permuted, inverse, axis=1)  108 us
    ppermute x2, waiting for transfers between devices, with_halo(): lax.ppermute(lax.slice_in_dim(block, block.shape[dim] - width, None, axis...  93.8 us
    ppermute x2, waiting for transfers between devices, with_halo(): lax.ppermute(lax.slice_in_dim(block, 0, width, axis=dim), axis, backward)  86.2 us
    unnamed x389, local copies, waits for them, and re-layouts  44.3 us
    psum x1, blocking collectives, body(): lax.psum(jnp.dot(resid, resid.T, precision=highest), ('bxy', 'bz'))  40.4 us
    psum x1, blocking collectives, body(): lax.psum(jnp.dot(basis, work.T, precision=highest), ('bxy', 'bz'))  38.9 us
  transfers between devices with their start and end apart: 6, of which 4 were waited for; matrix products, arithmetic and copies ran while one was open for 18% of the time, Pallas kernels for 0%

commit v1 on v0

v1 whole, which is shorter than its diff:
```python
import functools

import jax
import jax.numpy as jnp
from jax import lax
from jax.experimental import pallas as pl
from jax.experimental.pallas import tpu as pltpu
from jax.sharding import PartitionSpec as P

BLK = 16
KB = 48
CORES = 2
LANES = 128
VMEM_BYTES = 56 * 1024 * 1024


FLOW_DIRS = (
    (0, 0, 0),
    (1, 0, 0),
    (-1, 0, 0),
    (0, 1, 0),
    (0, -1, 0),
    (0, 0, 1),
    (0, 0, -1),
    (1, 1, 0),
    (-1, -1, 0),
    (1, -1, 0),
    (-1, 1, 0),
    (1, 0, 1),
    (-1, 0, -1),
    (1, 0, -1),
    (-1, 0, 1),
    (0, 1, 1),
    (0, -1, -1),
    (0, 1, -1),
    (0, -1, 1),
)
ALL_DIRS = FLOW_DIRS + FLOW_DIRS[:7]
FLOW_WEIGHTS = (1.0 / 3.0,) + (1.0 / 18.0,) * 6 + (1.0 / 36.0,) * 12
HEAT_WEIGHTS = (0.25,) + (0.125,) * 6
OPPOSITE = (0,) + tuple((number + 1 if number % 2 == 1 else number - 1 for number in range(1, 19)))
OMEGA_FLOW = 1.6
OMEGA_HEAT = 1.4
BUOYANCY = 0.2


def along(direction, comps):
    total = None
    for weight, array in zip(direction, comps):
        if weight == 1:
            total = array if total is None else total + array
        elif weight == -1:
            total = -array if total is None else total - array
    return total


def moments(flow, heat):
    density = flow[0]
    for number in range(1, 19):
        density = density + flow[number]
    momentum = []
    for comp in range(3):
        momentum.append(along([FLOW_DIRS[number][comp] for number in range(19)], flow))
    warmth = heat[0]
    for number in range(1, 7):
        warmth = warmth + heat[number]
    return (density, momentum, warmth)


def equilibria(density, momentum, warmth, velocity, temper):
    carried = [momentum[comp] - velocity[comp] * density for comp in range(3)]
    speed_sq = velocity[0] * velocity[0] + velocity[1] * velocity[1] + velocity[2] * velocity[2]
    carried_u = velocity[0] * carried[0] + velocity[1] * carried[1] + velocity[2] * carried[2]
    rest = density * (1.0 - 1.5 * speed_sq) - 3.0 * carried_u
    flow_eq = [FLOW_WEIGHTS[0] * rest] + [None] * 18
    heat_eq = [HEAT_WEIGHTS[0] * warmth] + [None] * 6
    for number in range(1, 19, 2):
        drift = along(FLOW_DIRS[number], velocity)
        push = along(FLOW_DIRS[number], carried)
        even = rest + drift * (4.5 * drift * density + 9.0 * push)
        odd = 3.0 * (drift * density + push)
        flow_eq[number] = FLOW_WEIGHTS[number] * (even + odd)
        flow_eq[number + 1] = FLOW_WEIGHTS[number] * (even - odd)
        if number < 7:
            tilt = 4.0 * (warmth * drift + temper * push)
            heat_eq[number] = HEAT_WEIGHTS[number] * (warmth + tilt)
            heat_eq[number + 1] = HEAT_WEIGHTS[number] * (warmth - tilt)
    return (flow_eq, heat_eq)


def lattice_kernel(count, high, fields_ref, base_ref, out_ref, first_ref, second_ref):
    wide = fields_ref.shape[2]

    def base_at(x):
        return (
            [base_ref[x, 0], base_ref[x, 1], base_ref[x, 2]],
            base_ref[x, 3],
            base_ref[x, 4] > 0.5,
        )

    def force(number, warmth):
        return 3.0 * FLOW_WEIGHTS[number] * FLOW_DIRS[number][1] * BUOYANCY * warmth

    def streamed(ref, x):
        found = []
        for number in range(26):
            first, second, third = ALL_DIRS[number]
            value = ref[number, lax.rem(x + count - first, count)]
            if second:
                value = pltpu.roll(value, second % wide, 0)
            if third:
                value = pltpu.roll(value, third % LANES, 1)
            found.append(value)
        return (found[:19], found[19:])

    def begin(x, carry):
        velocity, temper, solid = base_at(x)
        warmth = fields_ref[x, 4]
        flow, heat = equilibria(
            fields_ref[x, 0],
            [fields_ref[x, 1], fields_ref[x, 2], fields_ref[x, 3]],
            warmth,
            velocity,
            temper,
        )
        for number in range(19):
            fresh = flow[number]
            if FLOW_DIRS[number][1]:
                fresh = fresh + force(number, warmth)
            first_ref[number, x] = jnp.where(solid, flow[OPPOSITE[number]], fresh)
        for number in range(7):
            first_ref[19 + number, x] = jnp.where(solid, heat[OPPOSITE[number]], heat[number])
        return carry

    def again(x, carry):
        velocity, temper, solid = base_at(x)
        flow, heat = streamed(first_ref, x)
        density, momentum, warmth = moments(flow, heat)
        flow_eq, heat_eq = equilibria(density, momentum, warmth, velocity, temper)
        for number in range(19):
            fresh = (1.0 - OMEGA_FLOW) * flow[number] + OMEGA_FLOW * flow_eq[number]
            if FLOW_DIRS[number][1]:
                fresh = fresh + force(number, warmth)
            second_ref[number, x] = jnp.where(solid, flow[OPPOSITE[number]], fresh)
        for number in range(7):
            fresh = (1.0 - OMEGA_HEAT) * heat[number] + OMEGA_HEAT * heat_eq[number]
            second_ref[19 + number, x] = jnp.where(solid, heat[OPPOSITE[number]], fresh)
        return carry

    def finish(x, carry):
        flow, heat = streamed(second_ref, x)
        density, momentum, warmth = moments(flow, heat)
        for number, value in enumerate([density] + momentum + [warmth]):
            out_ref[x, number] = value[2 : 2 + high]
        return carry

    lax.fori_loop(0, count, begin, 0)
    lax.fori_loop(0, count, again, 0)
    lax.fori_loop(0, count, finish, 0)


def spread_kernel(piece, tall, order_ref, arrived_ref, mine_ref, other_ref, rows_ref, spread_ref):
    core = lax.rem(lax.axis_index("bz"), CORES)
    panels, vecs, padded = arrived_ref.shape
    step = 16 if piece % 16 == 0 else 8
    wide = mine_ref.shape[2]
    half = tall // CORES
    total = spread_ref.shape[0]

    def clear(i, carry):
        spread_ref[pl.ds(pl.multiple_of(i * 256, 256), 256), :] = jnp.zeros((256, LANES), jnp.float32)
        return carry

    lax.fori_loop(0, total // 256, clear, 0)

    def panel(i, carry):
        for start in range(0, padded, LANES):
            rows_ref[start : start + LANES, 0:vecs] = arrived_ref[i, :, start : start + LANES].T
        base = (CORES * i + core) * piece

        def rows(j, carry):
            at = pl.multiple_of(j * step, step)
            held = [rows_ref[pl.ds(at + t, 1), :] for t in range(step)]
            where = [order_ref[0, base + at + t] for t in range(step)]
            for t in range(step):
                spread_ref[pl.ds(where[t], 1), :] = held[t]
            return carry

        return lax.fori_loop(0, piece // step, rows, carry)

    lax.fori_loop(0, panels, panel, 0)

    for out_ref, which in ((mine_ref, core), (other_ref, 1 - core)):

        def moment(m, carry):
            for r in range(wide):
                level = lax.rem(half * which + tall - 2 + r, tall)
                start = pl.multiple_of((m * tall + level) * LANES, LANES)
                block = spread_ref[pl.ds(start, LANES), :].T
                for v in range(vecs):
                    out_ref[v, m, r : r + 1, :] = block[v : v + 1, :]
            return carry

        lax.fori_loop(0, 5, moment, 0)


def collect_kernel(piece, tall, order_ref, mine_ref, other_ref, out_ref, rows_ref, table_ref):
    core = lax.rem(lax.axis_index("bz"), CORES)
    panels, vecs, padded = out_ref.shape
    step = 16 if piece % 16 == 0 else 8
    half = tall // CORES

    for in_ref, which in ((mine_ref, core), (other_ref, 1 - core)):

        def moment(m, carry):
            for r in range(half):
                start = pl.multiple_of((m * tall + half * which + r) * LANES, LANES)
                block = jnp.concatenate([in_ref[v, m, r : r + 1, :] for v in range(vecs)], 0)
                table_ref[pl.ds(start, LANES), 0:vecs] = block.T
            return carry

        lax.fori_loop(0, 5, moment, 0)

    def panel(i, carry):
        base = (CORES * i + core) * piece

        def rows(j, carry):
            at = pl.multiple_of(j * step, step)
            where = [order_ref[0, base + at + t] for t in range(step)]
            held = [table_ref[pl.ds(where[t], 1), :] for t in range(step)]
            for t in range(step):
                rows_ref[pl.ds(at + t, 1), :] = held[t]
            return carry

        lax.fori_loop(0, piece // step, rows, 0)
        for start in range(0, padded, LANES):
            block = rows_ref[start : start + LANES, :].T
            out_ref[i, :, start : start + LANES] = block[0:vecs, :]
        return carry

    lax.fori_loop(0, panels, panel, 0)


def vmem():
    return pl.BlockSpec(memory_space=pltpu.VMEM)


def smem():
    return pl.BlockSpec(memory_space=pltpu.SMEM)


def params():
    return pltpu.CompilerParams(vmem_limit_bytes=VMEM_BYTES)


def swap_cores(array):
    count = lax.axis_size("bz")
    return lax.ppermute(array, "bz", [(i, i ^ 1) for i in range(count)])


def exchange(array):
    pairs = [[c + CORES * k for k in range(lax.axis_size("bz") // CORES)] for c in range(CORES)]
    array = lax.all_to_all(array, "bxy", split_axis=0, concat_axis=0, tiled=True)
    return lax.all_to_all(
        array, "bz", split_axis=1, concat_axis=1, tiled=True, axis_index_groups=pairs
    )


def body(basis, velocity, temper, flags, order):
    count_first = lax.axis_size("bxy")
    count_second = lax.axis_size("bz")
    devices = count_first * count_second
    panel_rows = basis.shape[1]
    piece = panel_rows // count_first
    slab_rows = piece * devices
    total_rows = panel_rows * devices
    tall, third = temper.shape[1:]
    ways = count_second // CORES
    vecs = BLK // ways
    parts = count_first // vecs
    high = tall // CORES // parts
    wide = -(-(tall // CORES + 4) // 8) * 8
    piece_wide = -(-(high + 4) // 8) * 8
    padded = -(-piece // LANES) * LANES
    panels = devices // CORES
    me_first = lax.axis_index("bxy")
    core = lax.rem(lax.axis_index("bz"), CORES)

    height = lax.broadcasted_iota(jnp.int32, temper.shape, 1)
    solid = (flags == 1) | (height == 0) | (height == tall - 1)
    base = jnp.concatenate([velocity, temper[None], solid.astype(jnp.float32)[None]], 0)
    base = base.transpose(1, 0, 2, 3)
    ring = jnp.concatenate([base[:, :, tall - 2 :], base, base[:, :, : wide]], 2)
    ring = lax.dynamic_slice_in_dim(ring, core * (tall // CORES), wide, 2)
    ring = lax.all_gather(ring, "bxy", axis=0, tiled=True)
    part = me_first // vecs
    if parts > 1:
        ring = jnp.concatenate([ring, ring[:, :, :8]], 2)
        ring = lax.dynamic_slice_in_dim(ring, part * high, piece_wide, 2)

    outgoing = basis[KB - BLK :].reshape(ways, vecs, count_first, piece).transpose(2, 0, 1, 3)
    outgoing = jnp.pad(outgoing, ((0, 0), (0, 0), (0, 0), (0, padded - piece)))
    arrived = exchange(outgoing).reshape(panels, vecs, padded)
    part_shape = jax.ShapeDtypeStruct((vecs, 5, wide, third), jnp.float32)
    mine, other = pl.pallas_call(
        functools.partial(spread_kernel, piece, tall),
        out_shape=(part_shape, part_shape),
        in_specs=[smem(), vmem()],
        out_specs=(vmem(), vmem()),
        scratch_shapes=[
            pltpu.VMEM((padded, LANES), jnp.float32),
            pltpu.VMEM((slab_rows, LANES), jnp.float32),
        ],
        compiler_params=params(),
    )(order, arrived)
    whole = mine + swap_cores(other)
    if parts > 1:
        whole = jnp.pad(whole, ((0, 0), (0, 0), (0, 8), (0, 0)))
        whole = jnp.concatenate(
            [whole[:, :, s * high : s * high + piece_wide] for s in range(parts)], 0
        )
    fields = lax.all_to_all(whole, "bxy", split_axis=0, concat_axis=0, tiled=True)

    state = pltpu.VMEM((26, count_first, piece_wide, third), jnp.float32)
    evolved = pl.pallas_call(
        functools.partial(lattice_kernel, count_first, high),
        out_shape=jax.ShapeDtypeStruct((count_first, 5, high, third), jnp.float32),
        in_specs=[vmem(), vmem()],
        out_specs=vmem(),
        scratch_shapes=[state, state],
        compiler_params=params(),
    )(fields, ring)

    back = lax.all_to_all(evolved, "bxy", split_axis=0, concat_axis=0, tiled=True)
    if parts > 1:
        back = (
            back.reshape(parts, vecs, 5, high, third)
            .transpose(1, 2, 0, 3, 4)
            .reshape(vecs, 5, parts * high, third)
        )
    leaving = pl.pallas_call(
        functools.partial(collect_kernel, piece, tall),
        out_shape=jax.ShapeDtypeStruct((panels, vecs, padded), jnp.float32),
        in_specs=[smem(), vmem(), vmem()],
        out_specs=vmem(),
        scratch_shapes=[
            pltpu.VMEM((padded, LANES), jnp.float32),
            pltpu.VMEM((slab_rows, LANES), jnp.float32),
        ],
        compiler_params=params(),
    )(order, back, swap_cores(back))
    landed = exchange(leaving.reshape(count_first, ways, vecs, padded))
    work = landed[..., :piece].transpose(1, 2, 0, 3).reshape(BLK, panel_rows)

    highest = lax.Precision.HIGHEST
    proj = lax.psum(jnp.dot(basis, work.T, precision=highest), ("bxy", "bz")) / total_rows
    resid = work - jnp.dot(proj.T, basis, precision=highest)
    gram = lax.psum(jnp.dot(resid, resid.T, precision=highest), ("bxy", "bz")) / total_rows
    lower = jnp.linalg.cholesky(gram)
    ortho = lax.linalg.triangular_solve(lower, resid, left_side=True, lower=True)
    return (ortho, proj, lower.T)


def solution(mesh):
    in_specs = (
        P(None, ("bxy", "bz")),
        P(None, "bxy", None, None),
        P("bxy", None, None),
        P("bxy", None, None),
        P("bxy", None),
    )
    out_specs = (P(None, ("bxy", "bz")), P(), P())
    return jax.shard_map(body, mesh=mesh, in_specs=in_specs, out_specs=out_specs, check_vma=False)
```

time: 871 us -> 286 us (0.33)
  local copies, waits for them, and re-layouts: 462 us -> 6.35 us
  waiting for transfers between devices: 188 us -> 4.17 us
  blocking collectives: 107 us -> 195 us
  other arithmetic: 80.7 us -> 6.22 us
  Pallas kernels: 0 us -> 64.2 us
  starting transfers between devices: 21.1 us -> 4.37 us
    gather x2 -> x0, local copies, waits for them, and re-layouts: 215 us -> none  [the longest x1 108 us: body(): reordered = jnp.take(evolved, permute, axis=1)]
    ppermute x4 -> x2, waiting for transfers between devices: 180 us -> 4.17 us  [swap_cores(): return lax.ppermute(array, 'bz', [(i, i ^ 1) for i in range(count)])]
    scatter x1 -> x0, local copies, waits for them, and re-layouts: 113 us -> none  [body(): jnp.zeros((slab_rows,), jnp.int32).at[permute]]
    pallas_call x0 -> x3, Pallas kernels: none -> 64.2 us  [the longest x1 30.4 us: body(): pl.pallas_call(functools.partial(spread_kernel, piece, tall), out_shape=(...]
    select_n x35 -> x0, other arithmetic: 58.1 us -> none  [the longest x1 18.2 us: body(): reordered = jnp.take(evolved, permute, axis=1)]
    all_to_all x2 -> x5, blocking collectives: 28.2 us -> 73.2 us  [the longest x2 40 us: exchange(): lax.all_to_all(array, 'bxy', split_axis=0, concat_axis=0, tiled=True)]
    all_gather x0 -> x1, blocking collectives: none -> 43 us  [body(): ring = lax.all_gather(ring, 'bxy', axis=0, tiled=True)]
    unnamed x389 -> x18, local copies, waits for them, and re-layouts: 44.3 us -> 3.39 us
  transfers between devices with their start and end apart: 6 -> 3, of which waited for: 4 -> 2; matrix products, arithmetic and copies ran while one was open for 18% -> 0% of each run, Pallas kernels for 0% -> 0%
where the time goes in v1:
time: 286 us
  blocking collectives  195 us (68%)
  Pallas kernels  64.2 us (22%)
  local copies, waits for them, and re-layouts  6.35 us (2%)
  other arithmetic  6.22 us (2%)
  starting transfers between devices  4.37 us (2%)
  matrix products  4.21 us (1%)
  waiting for transfers between devices  4.17 us (1%)
    all_gather x1, blocking collectives, body(): ring = lax.all_gather(ring, 'bxy', axis=0, tiled=True)  43 us
    psum x1, blocking collectives, body(): lax.psum(jnp.dot(resid, resid.T, precision=highest), ('bxy', 'bz'))  40.8 us
    all_to_all x2, blocking collectives, exchange(): lax.all_to_all(array, 'bxy', split_axis=0, concat_axis=0, tiled=True)  40 us
    psum x1, blocking collectives, body(): lax.psum(jnp.dot(basis, work.T, precision=highest), ('bxy', 'bz'))  38.3 us
    pallas_call x1, Pallas kernels, body(): pl.pallas_call(functools.partial(spread_kernel, piece, tall), out_shape=(...  30.4 us
    pallas_call x1, Pallas kernels, body(): pl.pallas_call(functools.partial(collect_kernel, piece, tall), out_shape=...  27.6 us
    all_to_all x2, blocking collectives, exchange(): lax.all_to_all(array, 'bz', split_axis=1, concat_axis=1, tiled=True, axis...  19.6 us
    all_to_all x1, blocking collectives, body(): lax.all_to_all(evolved, 'bxy', split_axis=0, concat_axis=0, tiled=True)  13.5 us
  transfers between devices with their start and end apart: 3, of which 2 were waited for; matrix products, arithmetic and copies ran while one was open for 0% of the time, Pallas kernels for 0%

profile of v1, /device:TPU:0, one launch (start us, length us, event | category | flops | bytes accessed | tf_op | source)
XLA Modules:
  0.0 285.6 jit_solution(8264766218143228180)
XLA Ops:
  0.6 1.1 slice.22
  1.7 0.3 reshape.27
  2.0 0.3 copy.39
  2.3 21.6 %all_to_all.30 = f32[8,2,8,1024]{3,2,1,0:T(8,128)S(1)} all-to-all(f32[8,2,8,1024]{3,2,1,0:T(8,128)S(1)} %pad.4.clone), channel_id=1, replica_groups=mesh['bxy'=8,'bz'=4] {'bxy'}, dimensions={0} | all-to-all | bytes 1048576 | tf_op jit(solution)/shard_map/all_to_all | solution.py:263
  24.0 9.5 %all_to_all.31 = f32[8,2,8,1024]{3,2,0,1:T(8,128)S(1)} all-to-all(f32[8,2,8,1024]{3,2,0,1:T(8,128)S(1)} %copy.30), channel_id=1, replica_groups={{0,2},{1,3},{4,6},{5,7},{8,10},{9,11},{12,14},{13,15},{16,18},{17,19},{..., dimensions={1} | all-to-all | bytes 1048576 | tf_op jit(solution)/shard_map/all_to_all | solution.py:264
  33.5 0.9 copy.31
  34.4 30.4 %shard_map.76 = (f32[8,5,32,128]{3,2,1,0:T(8,128)}, f32[8,5,32,128]{3,2,1,0:T(8,128)}) custom-call(s32[1,30720]{1,0:T(1,128)} %order_ref.3, f32[16,8,1024]{2,1,0:T(8,128)} %bitcast.34), custom_call_target="tpu_custom_call" | custom-call | tf_op jit(solution)/shard_map/pallas_call | solution.py:305
  64.8 0.0 collective-permute-start
  64.8 2.3 collective-permute-done
  67.1 0.0 copy-start.6
  67.1 0.0 copy-start.4
  67.1 0.0 copy-start.7
  67.1 2.1 add.23
  69.1 4.4 %all-to-all-start.2 = ((f32[8,5,32,128]{3,2,1,0:T(8,128)}), f32[8,5,32,128]{3,2,1,0:T(8,128)S(1)}, u32[]{:S(2)}, u32[]{:S(2)}) async-start(f32[8,5,32,128]{3,2,1,0:T(8,128)} %add.23), calls=%async_computation.2 | async-start | bytes 1310720 | tf_op jit(solution)/shard_map/all_to_all | solution.py:322
  73.5 0.0 copy-done.6
  73.5 0.1 convert_bitcast_fusion
  73.6 0.0 copy-done.4
  73.6 0.0 copy-done.7
  73.7 43.0 %all_gather.3.base_ref = f32[8,5,32,128]{3,2,1,0:T(8,128)} all-gather(f32[1,5,32,128]{3,2,1,0:T(8,128)S(1)} %fusion.1), channel_id=1, replica_groups=mesh['bxy'=8,'bz'=4] {'bxy'}, dimensions={0}, use_global_device_ids=true | all-gather | bytes 737280 | tf_op jit(solution)/shard_map/all_gather | solution.py:295
  116.7 0.0 all-to-all-done.2.fields_ref
  116.7 0.0 copy-start.1
  116.8 0.8 copy-done.1
  117.6 6.2 %shard_map.77 = f32[8,5,24,128]{3,2,1,0:T(8,128)} custom-call(f32[8,5,32,128]{3,2,1,0:T(8,128)} %copy-done.1, f32[8,5,32,128]{3,2,1,0:T(8,128)} %all_gather.3.base_ref), custom_call_target="tpu_custom_call" | custom-call | tf_op jit(solution)/shard_map/pallas_call | solution.py:325
  123.8 13.5 %all_to_all.32.mine_ref = f32[8,5,24,128]{3,2,1,0:T(8,128)S(1)} all-to-all(f32[8,5,24,128]{3,2,1,0:T(8,128)} %shard_map.77), channel_id=1, replica_groups=mesh['bxy'=8,'bz'=4] {'bxy'}, dimensions={0} | all-to-all | bytes 983040 | tf_op jit(solution)/shard_map/all_to_all | solution.py:334
  137.3 0.0 copy-start.2
  137.3 0.0 collective-permute-start.1
  137.3 1.9 collective-permute-done.1.other_ref
  139.1 0.0 copy-done.2
  139.2 0.0 copy-start.3
  139.2 0.8 copy-done.3
  139.9 27.6 %shard_map.78 = f32[16,8,1024]{2,1,0:T(8,128)} custom-call(s32[1,30720]{1,0:T(1,128)} %order_ref.3, f32[8,5,24,128]{3,2,1,0:T(8,128)} %copy-done.2, f32[8,5,24,128]{3,2,1,0:T(8,128)} %copy-done.3), custom_call_target="tpu_custom_call" | custom-call | tf_op jit(solution)/shard_map/pallas_call | solution.py:341
  167.5 18.5 %all_to_all.33 = f32[8,2,8,1024]{3,2,1,0:T(8,128)S(1)} all-to-all(f32[8,2,8,1024]{3,2,1,0:T(8,128)} %bitcast.33), channel_id=1, replica_groups=mesh['bxy'=8,'bz'=4] {'bxy'}, dimensions={0} | all-to-all | bytes 1048576 | tf_op jit(solution)/shard_map/all_to_all | solution.py:263
  186.0 10.1 %all_to_all.34 = f32[8,2,8,1024]{3,2,0,1:T(8,128)S(1)} all-to-all(f32[8,2,8,1024]{3,2,0,1:T(8,128)S(1)} %copy.33), channel_id=1, replica_groups={{0,2},{1,3},{4,6},{5,7},{8,10},{9,11},{12,14},{13,15},{16,18},{17,19},{..., dimensions={1} | all-to-all | bytes 1048576 | tf_op jit(solution)/shard_map/all_to_all | solution.py:264
  196.1 0.0 copy-start
  196.1 0.3 copy.34
  196.5 0.2 reshape.30
  196.7 0.8 copy-done
  197.5 1.2 convolution_bitcast_fusion
  198.7 38.3 %psum.14 = f32[48,16]{0,1:T(8,128)S(1)} all-reduce(f32[48,16]{0,1:T(8,128)S(1)} %convolution_bitcast_fusion), channel_id=1, replica_groups=mesh['bxy'=8,'bz'=4] {'bxy','bz'}, use_global_device_ids=true, to_apply=%region_0.1 | all-reduce | flops 768 | bytes 6144 | tf_op jit(solution)/shard_map/psum | solution.py:356
  237.1 0.0 copy-start.5
  237.1 0.8 convolution_subtract_fusion
  237.9 0.8 fusion.6
  238.6 0.0 copy-done.5
  238.6 40.8 %psum.15 = f32[16,16]{0,1:T(8,128)S(1)} all-reduce(f32[16,16]{0,1:T(8,128)S(1)} %fusion.6), channel_id=1, replica_groups=mesh['bxy'=8,'bz'=4] {'bxy','bz'}, use_global_device_ids=true, to_apply=%region_1.2 | all-reduce | flops 256 | bytes 2048 | tf_op jit(solution)/shard_map/psum | solution.py:358
  279.4 0.1 copy.36
  279.5 1.5 cholesky.16
  281.0 0.6 compare_reduce_fusion
  281.6 0.6 fusion.5
  282.3 1.2 custom-call.6
  283.5 1.4 fusion.2
  284.9 0.7 copy.37
  (13 shorter events, 0.3 us)
Async XLA Ops:
  64.8 2.3 collective-permute-start
  67.1 6.4 %copy-start.6 = (s32[1,48,128]{2,1,0:T(8,128)S(1)}, s32[1,48,128]{2,1,0:T(8,128)}, u32[]{:S(2)}) copy-start(s32[1,48,128]{2,1,0:T(8,128)} %param.8) | copy-start | bytes 73732
  67.1 6.5 %copy-start.4 = (f32[3,1,48,128]{3,2,1,0:T(8,128)S(1)}, f32[3,1,48,128]{3,2,1,0:T(8,128)}, u32[]{:S(2)}) copy-start(f32[3,1,48,128]{3,2,1,0:T(8,128)} %param.6) | copy-start | bytes 221188
  67.1 6.5 %copy-start.7 = (f32[1,48,128]{2,1,0:T(8,128)S(1)}, f32[1,48,128]{2,1,0:T(8,128)}, u32[]{:S(2)}) copy-start(f32[1,48,128]{2,1,0:T(8,128)} %param.7) | copy-start | bytes 73732
  69.1 47.6 %all-to-all-start.2 = ((f32[8,5,32,128]{3,2,1,0:T(8,128)}), f32[8,5,32,128]{3,2,1,0:T(8,128)S(1)}, u32[]{:S(2)}, u32[]{:S(2)}) async-start(f32[8,5,32,128]{3,2,1,0:T(8,128)} %add.23), calls=%async_computation.2 | async-start | bytes 1310720 | tf_op jit(solution)/shard_map/all_to_all | solution.py:322
  116.7 0.8 copy-start.1
  137.3 1.9 copy-start.2
  137.3 1.9 collective-permute-start.1
  139.2 0.8 copy-start.3
  196.1 1.4 copy-start
  237.1 1.6 copy-start.5

commit v2 on v1

--- a/solution.py
+++ b/solution.py
@@ -241,6 +241,254 @@
     lax.fori_loop(0, panels, panel, 0)
 
 
+def exchange_start(send, out_ref, sends, recvs, me, count, place):
+    def start(d, carry):
+        to = lax.rem(me + d, count)
+        remote(send.at[to], out_ref.at[me], sends.at[to], recvs.at[me], place(to)).start()
+        return carry
+
+    lax.fori_loop(1, count, start, 0)
+
+
+def exchange_wait(send, out_ref, sends, recvs, me, count, place, then=None):
+    def wait(d, carry):
+        source = lax.rem(me + count - d, count)
+        remote(send.at[source], out_ref.at[source], sends.at[source], recvs.at[source], place(source)).wait_recv()
+        if then is not None:
+            then(source)
+        return carry
+
+    lax.fori_loop(1, count, wait, 0)
+
+
+def exchange_drain(send, out_ref, sends, recvs, me, count, place):
+    def drain(d, carry):
+        to = lax.rem(me + d, count)
+        remote(send.at[to], out_ref.at[me], sends.at[to], recvs.at[me], place(to)).wait_send()
+        return carry
+
+    lax.fori_loop(1, count, drain, 0)
+
+
+def remote(source, target, send, recv, place):
+    return pltpu.make_async_remote_copy(
+        src_ref=source,
+        dst_ref=target,
+        send_sem=send,
+        recv_sem=recv,
+        device_id=place,
+        device_id_type=pl.DeviceIdType.MESH,
+    )
+
+
+def greet(me, count, place):
+    barrier = pltpu.get_barrier_semaphore()
+
+    def hello(d, carry):
+        pl.semaphore_signal(
+            barrier, inc=1, device_id=place(lax.rem(me + d, count)), device_id_type=pl.DeviceIdType.MESH
+        )
+        return carry
+
+    lax.fori_loop(1, count, hello, 0)
+
+
+def position():
+    first, second = lax.axis_index("bxy"), lax.axis_index("bz")
+    return (first, second, lax.rem(second, CORES), second // CORES)
+
+
+def panels_kernel(ways, outgoing_ref, arrived_ref, sends, recvs):
+    first, _, core, way = position()
+    count = outgoing_ref.shape[0]
+    me = first * ways + way
+
+    def place(i):
+        return (i // ways, lax.rem(i, ways) * CORES + core)
+
+    greet(me, count, place)
+    pl.semaphore_wait(pltpu.get_barrier_semaphore(), count - 1)
+    group = (outgoing_ref, arrived_ref, sends, recvs, me, count, place)
+    exchange_start(*group)
+    arrived_ref[me] = outgoing_ref[me]
+    exchange_wait(*group)
+    exchange_drain(*group)
+
+
+def gather_kernel(mine_ref, other_ref, out_ref, got_ref, mix_ref, swap_s, swap_r, sends, recvs):
+    me, second, core, _ = position()
+    count = mine_ref.shape[0]
+    sibling = (me, second + 1 - 2 * core)
+
+    def place(i):
+        return (i, second)
+
+    greet(me, count, place)
+    barrier = pltpu.get_barrier_semaphore()
+    pl.semaphore_signal(barrier, inc=1, device_id=sibling, device_id_type=pl.DeviceIdType.MESH)
+    pl.semaphore_wait(barrier, count)
+
+    def swap(i):
+        return remote(other_ref.at[i], got_ref.at[i], swap_s.at[i], swap_r.at[i], sibling)
+
+    def begin(d, carry):
+        swap(lax.rem(me + d, count)).start()
+        return carry
+
+    lax.fori_loop(1, count + 1, begin, 0)
+
+    def send(d, carry):
+        to = lax.rem(me + d, count)
+        swap(to).wait_recv()
+        mix_ref[to] = mine_ref[to] + got_ref[to]
+        remote(mix_ref.at[to], out_ref.at[me], sends.at[to], recvs.at[me], place(to)).start()
+        return carry
+
+    lax.fori_loop(1, count, send, 0)
+    swap(me).wait_recv()
+    out_ref[me] = mine_ref[me] + got_ref[me]
+    group = (mix_ref, out_ref, sends, recvs, me, count, place)
+    exchange_wait(*group)
+    exchange_drain(*group)
+
+    def end(i, carry):
+        swap(i).wait_send()
+        return carry
+
+    lax.fori_loop(0, count, end, 0)
+
+
+def scatter_kernel(evolved_ref, mine_ref, other_ref, swap_s, swap_r, sends, recvs):
+    me, second, core, _ = position()
+    count = evolved_ref.shape[0]
+    sibling = (me, second + 1 - 2 * core)
+
+    def place(i):
+        return (i, second)
+
+    greet(me, count, place)
+    barrier = pltpu.get_barrier_semaphore()
+    pl.semaphore_signal(barrier, inc=1, device_id=sibling, device_id_type=pl.DeviceIdType.MESH)
+    pl.semaphore_wait(barrier, count)
+
+    def swap(i):
+        return remote(mine_ref.at[i], other_ref.at[i], swap_s.at[i], swap_r.at[i], sibling)
+
+    group = (evolved_ref, mine_ref, sends, recvs, me, count, place)
+    exchange_start(*group)
+    mine_ref[me] = evolved_ref[me]
+    swap(me).start()
+    exchange_wait(*group, then=lambda source: swap(source).start())
+    exchange_drain(*group)
+
+    def end(i, carry):
+        swap(i).wait()
+        return carry
+
+    lax.fori_loop(0, count, end, 0)
+
+
+def project_kernel(
+    ways, piece, total_rows, leaving_ref, basis_ref, ortho_ref, proj_ref, upper_ref,
+    landed_ref, stack_ref, near_ref, far_ref, sends, recvs, near_s, near_r, far_s, far_r,
+):
+    first, second, core, way = position()
+    count = leaving_ref.shape[0]
+    count_second, count_first = near_ref.shape[0], far_ref.shape[0]
+    vecs = BLK // ways
+    me = first * ways + way
+
+    def place(i):
+        return (i // ways, lax.rem(i, ways) * CORES + core)
+
+    greet(me, count, place)
+    barrier = pltpu.get_barrier_semaphore()
+    for k in range(ways):
+        pl.semaphore_signal(
+            barrier, inc=1, device_id=(first, k * CORES + 1 - core), device_id_type=pl.DeviceIdType.MESH
+        )
+    pl.semaphore_wait(barrier, count - 1 + ways)
+    group = (leaving_ref, landed_ref, sends, recvs, me, count, place)
+    exchange_start(*group)
+    landed_ref[me] = leaving_ref[me]
+    stack_ref[0:KB] = basis_ref[...]
+    exchange_wait(*group)
+    for p in range(count_first):
+        for k in range(ways):
+            stack_ref[KB + k * vecs : KB + (k + 1) * vecs, p * piece : (p + 1) * piece] = landed_ref[
+                p * ways + k, :, 0:piece
+            ]
+    highest = lax.Precision.HIGHEST
+    across = (((1,), (1,)), ((), ()))
+    stack = stack_ref[...]
+    inner = lax.dot_general(stack, stack, across, precision=highest, preferred_element_type=jnp.float32)
+
+    near_ref[second] = jnp.concatenate([inner[0:32], inner[32:64]], 1)
+    group_near = (near_ref, near_ref, near_s, near_r, second, count_second, lambda i: (first, i))
+    share(*group_near)
+    summed = near_ref[0]
+    for i in range(1, count_second):
+        summed = summed + near_ref[i]
+    far_ref[first] = summed
+    group_far = (far_ref, far_ref, far_s, far_r, first, count_first, lambda i: (i, second))
+    share(*group_far)
+    summed = far_ref[0]
+    for i in range(1, count_first):
+        summed = summed + far_ref[i]
+    summed = summed * (1.0 / total_rows)
+    inner = jnp.concatenate([summed[:, 0:64], summed[:, 64:128]], 0)
+    proj = inner[0:KB, KB:]
+    proj_ref[...] = proj
+    mixed = inner[KB:, 0:KB]
+    twice = 2.0 * proj - jnp.dot(inner[0:KB, 0:KB], proj, precision=highest, preferred_element_type=jnp.float32)
+    gram = inner[KB:, KB:] - jnp.dot(mixed, twice, precision=highest, preferred_element_type=jnp.float32)
+
+    row_at = lax.broadcasted_iota(jnp.int32, (BLK, LANES), 0)
+    lane_at = lax.broadcasted_iota(jnp.int32, (BLK, LANES), 1)
+    unit = jnp.where(row_at == lane_at, 1.0, 0.0)
+    left = jnp.concatenate(
+        [gram, -mixed, unit[:, 0:BLK], jnp.zeros((BLK, LANES - 2 * BLK - KB), jnp.float32)], 1
+    )
+    solved = jnp.zeros((BLK, LANES), jnp.float32)
+    for j in range(BLK):
+        pivot = jnp.sqrt(left[j : j + 1, j : j + 1])
+        row = left[j : j + 1, :] / pivot
+        column = left[:, j : j + 1] / pivot
+        solved = jnp.where(row_at == j, row, solved)
+        left = left - jnp.where(row_at > j, column * row, 0.0)
+    upper_ref[...] = jnp.where(lane_at >= row_at, solved, 0.0)[:, 0:BLK]
+    ortho_ref[...] = jnp.dot(
+        solved[:, BLK : 2 * BLK + KB], stack_ref[...], precision=highest, preferred_element_type=jnp.float32
+    )
+    exchange_drain(*group)
+    drain_share(*group_near)
+    drain_share(*group_far)
+
+
+def share(held, _, sends, recvs, me, count, place):
+    def start(d, carry):
+        to = lax.rem(me + d, count)
+        remote(held.at[me], held.at[me], sends.at[to], recvs.at[me], place(to)).start()
+        return carry
+
+    def wait(d, carry):
+        source = lax.rem(me + count - d, count)
+        remote(held.at[source], held.at[source], sends.at[source], recvs.at[source], place(source)).wait_recv()
+        return carry
+
+    lax.fori_loop(1, count, start, 0)
+    lax.fori_loop(1, count, wait, 0)
+
+
+def drain_share(held, _, sends, recvs, me, count, place):
+    def drain(d, carry):
+        to = lax.rem(me + d, count)
+        remote(held.at[me], held.at[me], sends.at[to], recvs.at[me], place(to)).wait_send()
+        return carry
+
+    lax.fori_loop(1, count, drain, 0)
+
+
 def vmem():
     return pl.BlockSpec(memory_space=pltpu.VMEM)
 
@@ -249,21 +497,20 @@
     return pl.BlockSpec(memory_space=pltpu.SMEM)
 
 
-def params():
-    return pltpu.CompilerParams(vmem_limit_bytes=VMEM_BYTES)
-
-
-def swap_cores(array):
-    count = lax.axis_size("bz")
-    return lax.ppermute(array, "bz", [(i, i ^ 1) for i in range(count)])
-
-
-def exchange(array):
-    pairs = [[c + CORES * k for k in range(lax.axis_size("bz") // CORES)] for c in range(CORES)]
-    array = lax.all_to_all(array, "bxy", split_axis=0, concat_axis=0, tiled=True)
-    return lax.all_to_all(
-        array, "bz", split_axis=1, concat_axis=1, tiled=True, axis_index_groups=pairs
+def params(collective=None):
+    if collective is None:
+        return pltpu.CompilerParams(vmem_limit_bytes=VMEM_BYTES)
+    return pltpu.CompilerParams(
+        vmem_limit_bytes=VMEM_BYTES, collective_id=collective, has_side_effects=True
     )
+
+
+def cost(micros):
+    return pl.CostEstimate(flops=0, bytes_accessed=int(micros * 3.6e6), transcendentals=0)
+
+
+def semaphores(count, pairs):
+    return [pltpu.SemaphoreType.DMA((count,))] * (2 * pairs)
 
 
 def body(basis, velocity, temper, flags, order):
@@ -300,7 +547,16 @@
 
     outgoing = basis[KB - BLK :].reshape(ways, vecs, count_first, piece).transpose(2, 0, 1, 3)
     outgoing = jnp.pad(outgoing, ((0, 0), (0, 0), (0, 0), (0, padded - piece)))
-    arrived = exchange(outgoing).reshape(panels, vecs, padded)
+    outgoing = outgoing.reshape(panels, vecs, padded)
+    arrived = pl.pallas_call(
+        functools.partial(panels_kernel, ways),
+        out_shape=jax.ShapeDtypeStruct((panels, vecs, padded), jnp.float32),
+        in_specs=[vmem()],
+        out_specs=vmem(),
+        scratch_shapes=semaphores(panels, 1),
+        compiler_params=params(0),
+        cost_estimate=cost(12),
+    )(outgoing)
     part_shape = jax.ShapeDtypeStruct((vecs, 5, wide, third), jnp.float32)
     mine, other = pl.pallas_call(
         functools.partial(spread_kernel, piece, tall),
@@ -312,14 +568,23 @@
             pltpu.VMEM((slab_rows, LANES), jnp.float32),
         ],
         compiler_params=params(),
+        cost_estimate=cost(28),
     )(order, arrived)
-    whole = mine + swap_cores(other)
     if parts > 1:
-        whole = jnp.pad(whole, ((0, 0), (0, 0), (0, 8), (0, 0)))
-        whole = jnp.concatenate(
-            [whole[:, :, s * high : s * high + piece_wide] for s in range(parts)], 0
-        )
-    fields = lax.all_to_all(whole, "bxy", split_axis=0, concat_axis=0, tiled=True)
+        mine, other = [
+            jnp.concatenate([array[:, :, s * high : s * high + piece_wide] for s in range(parts)], 0)
+            for array in (mine, other)
+        ]
+    block = (count_first, 5, piece_wide, third)
+    fields = pl.pallas_call(
+        gather_kernel,
+        out_shape=jax.ShapeDtypeStruct(block, jnp.float32),
+        in_specs=[vmem(), vmem()],
+        out_specs=vmem(),
+        scratch_shapes=[pltpu.VMEM(block, jnp.float32)] * 2 + semaphores(count_first, 2),
+        compiler_params=params(1),
+        cost_estimate=cost(12),
+    )(mine, other)
 
     state = pltpu.VMEM((26, count_first, piece_wide, third), jnp.float32)
     evolved = pl.pallas_call(
@@ -331,13 +596,23 @@
         compiler_params=params(),
     )(fields, ring)
 
-    back = lax.all_to_all(evolved, "bxy", split_axis=0, concat_axis=0, tiled=True)
+    half_shape = jax.ShapeDtypeStruct((count_first, 5, high, third), jnp.float32)
+    back, back_other = pl.pallas_call(
+        scatter_kernel,
+        out_shape=(half_shape, half_shape),
+        in_specs=[vmem()],
+        out_specs=(vmem(), vmem()),
+        scratch_shapes=semaphores(count_first, 2),
+        compiler_params=params(2),
+        cost_estimate=cost(12),
+    )(evolved)
     if parts > 1:
-        back = (
-            back.reshape(parts, vecs, 5, high, third)
+        back, back_other = [
+            array.reshape(parts, vecs, 5, high, third)
             .transpose(1, 2, 0, 3, 4)
             .reshape(vecs, 5, parts * high, third)
-        )
+            for array in (back, back_other)
+        ]
     leaving = pl.pallas_call(
         functools.partial(collect_kernel, piece, tall),
         out_shape=jax.ShapeDtypeStruct((panels, vecs, padded), jnp.float32),
@@ -348,17 +623,29 @@
             pltpu.VMEM((slab_rows, LANES), jnp.float32),
         ],
         compiler_params=params(),
-    )(order, back, swap_cores(back))
-    landed = exchange(leaving.reshape(count_first, ways, vecs, padded))
-    work = landed[..., :piece].transpose(1, 2, 0, 3).reshape(BLK, panel_rows)
-
-    highest = lax.Precision.HIGHEST
-    proj = lax.psum(jnp.dot(basis, work.T, precision=highest), ("bxy", "bz")) / total_rows
-    resid = work - jnp.dot(proj.T, basis, precision=highest)
-    gram = lax.psum(jnp.dot(resid, resid.T, precision=highest), ("bxy", "bz")) / total_rows
-    lower = jnp.linalg.cholesky(gram)
-    ortho = lax.linalg.triangular_solve(lower, resid, left_side=True, lower=True)
-    return (ortho, proj, lower.T)
+        cost_estimate=cost(28),
+    )(order, back, back_other)
+    return pl.pallas_call(
+        functools.partial(project_kernel, ways, piece, total_rows),
+        out_shape=(
+            jax.ShapeDtypeStruct((BLK, panel_rows), jnp.float32),
+            jax.ShapeDtypeStruct((KB, BLK), jnp.float32),
+            jax.ShapeDtypeStruct((BLK, BLK), jnp.float32),
+        ),
+        in_specs=[vmem(), vmem()],
+        out_specs=(vmem(), vmem(), vmem()),
+        scratch_shapes=[
+            pltpu.VMEM((panels, vecs, padded), jnp.float32),
+            pltpu.VMEM((KB + BLK, panel_rows), jnp.float32),
+            pltpu.VMEM((count_second, 32, LANES), jnp.float32),
+            pltpu.VMEM((count_first, 32, LANES), jnp.float32),
+        ]
+        + semaphores(panels, 1)
+        + semaphores(count_second, 1)
+        + semaphores(count_first, 1),
+        compiler_params=params(3),
+        cost_estimate=cost(20),
+    )(leaving, basis)
 
 
 def solution(mesh):

time: 286 us -> 198 us (0.69)
  blocking collectives: 195 us -> 36.7 us
  Pallas kernels: 64.2 us -> 153 us
  other arithmetic: 6.22 us -> 0.14 us
  starting transfers between devices: 4.37 us -> 0 us
  matrix products: 4.21 us -> 0 us
  waiting for transfers between devices: 4.17 us -> 0 us
    pallas_call x0 -> x4, Pallas kernels: none -> 88.9 us  [the longest x1 35.3 us: body(): pl.pallas_call(functools.partial(project_kernel, ways, piece, total_rows)...]
    psum x2 -> x0, blocking collectives: 79.1 us -> none  [the longest x1 40.8 us: body(): lax.psum(jnp.dot(resid, resid.T, precision=highest), ('bxy', 'bz'))]
    all_to_all x5 -> x0, blocking collectives: 73.2 us -> none  [the longest x2 40 us: exchange(): lax.all_to_all(array, 'bxy', split_axis=0, concat_axis=0, tiled=True)]
    all_gather x1, blocking collectives: 43 us -> 36.7 us  [body(): ring = lax.all_gather(ring, 'bxy', axis=0, tiled=True)]
    all_to_all x1 -> x0, starting transfers between devices: 4.37 us -> none  [body(): lax.all_to_all(whole, 'bxy', split_axis=0, concat_axis=0, tiled=True)]
    ppermute x2 -> x0, waiting for transfers between devices: 4.17 us -> none  [swap_cores(): return lax.ppermute(array, 'bz', [(i, i ^ 1) for i in range(count)])]
    another operation x4 -> x0, other arithmetic: 3.36 us -> none  [the longest x3 2.13 us: body(): lower = jnp.linalg.cholesky(gram)]
  transfers between devices with their start and end apart: 3 -> 0, of which waited for: 2 -> 0; matrix products, arithmetic and copies ran while one was open for 0% -> 0% of each run, Pallas kernels for 0% -> 0%
where the time goes in v2:
time: 198 us
  Pallas kernels  153 us (77%)
  blocking collectives  36.7 us (19%)
  local copies, waits for them, and re-layouts  7.04 us (4%)
    all_gather x1, blocking collectives, body(): ring = lax.all_gather(ring, 'bxy', axis=0, tiled=True)  36.7 us
    pallas_call x1, Pallas kernels, body(): pl.pallas_call(functools.partial(project_kernel, ways, piece, total_rows)...  35.3 us
    pallas_call x1, Pallas kernels, body(): pl.pallas_call(functools.partial(spread_kernel, piece, tall), out_shape=(...  30.5 us
    pallas_call x1, Pallas kernels, body(): pl.pallas_call(functools.partial(collect_kernel, piece, tall), out_shape=...  27.6 us
    pallas_call x1, Pallas kernels, body(): pl.pallas_call(gather_kernel, out_shape=jax.ShapeDtypeStruct(block, jnp.f...  20.3 us
    pallas_call x1, Pallas kernels, body(): pl.pallas_call(functools.partial(panels_kernel, ways), out_shape=jax.Shap...  17.5 us
    pallas_call x1, Pallas kernels, body(): pl.pallas_call(scatter_kernel, out_shape=(half_shape, half_shape), in_spe...  15.8 us
    pallas_call x1, Pallas kernels, body(): pl.pallas_call(functools.partial(lattice_kernel, count_first, high), out_...  6.19 us

profile of v2, /device:TPU:0, one launch (start us, length us, event | category | flops | bytes accessed | tf_op | source)
XLA Modules:
  0.0 197.9 jit_solution(6850496784443934208)
XLA Ops:
  0.6 1.1 slice.9
  1.7 0.3 reshape.12
  2.0 0.3 copy.15
  2.3 0.8 pad.4
  3.1 17.5 %shard_map.76.arrived_ref = f32[16,8,1024]{2,1,0:T(8,128)} custom-call(f32[16,8,1024]{2,1,0:T(8,128)} %bitcast.11), custom_call_target="tpu_custom_call" | custom-call | bytes 43200000 | tf_op jit(solution)/shard_map/pallas_call | solution.py:551
  20.6 0.0 copy-start.1
  20.6 0.0 copy-start
  20.6 0.0 copy-start.2
  20.6 30.5 %shard_map.77 = (f32[8,5,32,128]{3,2,1,0:T(8,128)}, f32[8,5,32,128]{3,2,1,0:T(8,128)}) custom-call(s32[1,30720]{1,0:T(1,128)} %order_ref.3, f32[16,8,1024]{2,1,0:T(8,128)} %shard_map.76.arrived_ref), custom_call_target="tpu_custom_call" | custom-call | bytes 100800000 | tf_op jit(solution)/shard_map/pallas_call | solution.py:561
  51.2 20.3 %shard_map.78.fields_ref = f32[8,5,32,128]{3,2,1,0:T(8,128)} custom-call(f32[8,5,32,128]{3,2,1,0:T(8,128)} %get-tuple-element.7.mine_ref, f32[8,5,32,128]{3,2,1,0:T(8,128)} %get-tuple-element.8.other_ref), custom_call_target="tpu_custom_call" | custom-call | bytes 43200000 | tf_op jit(solution)/shard_map/pallas_call | solution.py:579
  71.5 0.0 copy-done.1
  71.5 0.1 convert_bitcast_fusion
  71.6 0.0 copy-done
  71.6 0.0 copy-done.2
  71.7 36.7 %all_gather.3.base_ref = f32[8,5,32,128]{3,2,1,0:T(8,128)} all-gather(f32[1,5,32,128]{3,2,1,0:T(8,128)S(1)} %fusion.1), channel_id=1, replica_groups=mesh['bxy'=8,'bz'=4] {'bxy'}, dimensions={0}, use_global_device_ids=true | all-gather | bytes 737280 | tf_op jit(solution)/shard_map/all_gather | solution.py:542
  108.4 6.2 %shard_map.79.evolved_ref = f32[8,5,24,128]{3,2,1,0:T(8,128)} custom-call(f32[8,5,32,128]{3,2,1,0:T(8,128)} %shard_map.78.fields_ref, f32[8,5,32,128]{3,2,1,0:T(8,128)} %all_gather.3.base_ref), custom_call_target="tpu_custom_call" | custom-call | tf_op jit(solution)/shard_map/pallas_call | solution.py:590
  114.6 15.8 %shard_map.80 = (f32[8,5,24,128]{3,2,1,0:T(8,128)}, f32[8,5,24,128]{3,2,1,0:T(8,128)}) custom-call(f32[8,5,24,128]{3,2,1,0:T(8,128)} %shard_map.79.evolved_ref), custom_call_target="tpu_custom_call" | custom-call | bytes 43200000 | tf_op jit(solution)/shard_map/pallas_call | solution.py:600
  130.5 27.6 %shard_map.81.leaving_ref = f32[16,8,1024]{2,1,0:T(8,128)} custom-call(s32[1,30720]{1,0:T(1,128)} %order_ref.3, f32[8,5,24,128]{3,2,1,0:T(8,128)} %get-tuple-element.9.mine_ref, f32[8,5,24,128]{3,2,1,0:T(8,128)} %get-tuple-element.10.other_ref), custom_call_target="tpu_custom_call" | custom-call | bytes 100800000 | tf_op jit(solution)/shard_map/pallas_call | solution.py:616
  158.0 35.3 %shard_map.82 = (f32[16,7680]{1,0:T(8,128)}, f32[48,16]{1,0:T(8,128)}, f32[16,16]{1,0:T(8,128)}) custom-call(f32[16,8,1024]{2,1,0:T(8,128)} %shard_map.81.leaving_ref, f32[48,7680]{1,0:T(8,128)} %basis_ref.1), custom_call_target="tpu_custom_call" | custom-call | bytes 72000000 | tf_op jit(solution)/shard_map/pallas_call | solution.py:628
  193.3 1.4 copy.13
  194.7 1.8 copy.18
  196.6 1.3 copy.19
  (5 shorter events, 0.1 us)
Async XLA Ops:
  20.6 50.9 %copy-start.1 = (s32[1,48,128]{2,1,0:T(8,128)S(1)}, s32[1,48,128]{2,1,0:T(8,128)}, u32[]{:S(2)}) copy-start(s32[1,48,128]{2,1,0:T(8,128)} %param.8) | copy-start | bytes 73732
  20.6 51.0 %copy-start = (f32[3,1,48,128]{3,2,1,0:T(8,128)S(1)}, f32[3,1,48,128]{3,2,1,0:T(8,128)}, u32[]{:S(2)}) copy-start(f32[3,1,48,128]{3,2,1,0:T(8,128)} %param.6) | copy-start | bytes 221188
  20.6 51.0 %copy-start.2 = (f32[1,48,128]{2,1,0:T(8,128)S(1)}, f32[1,48,128]{2,1,0:T(8,128)}, u32[]{:S(2)}) copy-start(f32[1,48,128]{2,1,0:T(8,128)} %param.7) | copy-start | bytes 73732

commit v3 on v2

--- a/solution.py
+++ b/solution.py
@@ -91,7 +91,10 @@
 def lattice_kernel(count, high, fields_ref, base_ref, out_ref, first_ref, second_ref):
     wide = fields_ref.shape[2]
 
-    def base_at(x):
+    me = lax.axis_index("bxy")
+
+    def base_at(place):
+        x = lax.rem(me + count - place, count)
         return (
             [base_ref[x, 0], base_ref[x, 1], base_ref[x, 2]],
             base_ref[x, 3],
@@ -162,7 +165,7 @@
 def spread_kernel(piece, tall, order_ref, arrived_ref, mine_ref, other_ref, rows_ref, spread_ref):
     core = lax.rem(lax.axis_index("bz"), CORES)
     panels, vecs, padded = arrived_ref.shape
-    step = 16 if piece % 16 == 0 else 8
+    step = next(size for size in (48, 40, 32, 16, 8) if piece % size == 0)
     wide = mine_ref.shape[2]
     half = tall // CORES
     total = spread_ref.shape[0]
@@ -179,11 +182,10 @@
         base = (CORES * i + core) * piece
 
         def rows(j, carry):
-            at = pl.multiple_of(j * step, step)
+            at = pl.multiple_of(j * step, 8)
             held = [rows_ref[pl.ds(at + t, 1), :] for t in range(step)]
-            where = [order_ref[0, base + at + t] for t in range(step)]
             for t in range(step):
-                spread_ref[pl.ds(where[t], 1), :] = held[t]
+                spread_ref[pl.ds(order_ref[0, base + at + t], 1), :] = held[t]
             return carry
 
         return lax.fori_loop(0, piece // step, rows, carry)
@@ -202,43 +204,6 @@
             return carry
 
         lax.fori_loop(0, 5, moment, 0)
-
-
-def collect_kernel(piece, tall, order_ref, mine_ref, other_ref, out_ref, rows_ref, table_ref):
-    core = lax.rem(lax.axis_index("bz"), CORES)
-    panels, vecs, padded = out_ref.shape
-    step = 16 if piece % 16 == 0 else 8
-    half = tall // CORES
-
-    for in_ref, which in ((mine_ref, core), (other_ref, 1 - core)):
-
-        def moment(m, carry):
-            for r in range(half):
-                start = pl.multiple_of((m * tall + half * which + r) * LANES, LANES)
-                block = jnp.concatenate([in_ref[v, m, r : r + 1, :] for v in range(vecs)], 0)
-                table_ref[pl.ds(start, LANES), 0:vecs] = block.T
-            return carry
-
-        lax.fori_loop(0, 5, moment, 0)
-
-    def panel(i, carry):
-        base = (CORES * i + core) * piece
-
-        def rows(j, carry):
-            at = pl.multiple_of(j * step, step)
-            where = [order_ref[0, base + at + t] for t in range(step)]
-            held = [table_ref[pl.ds(where[t], 1), :] for t in range(step)]
-            for t in range(step):
-                rows_ref[pl.ds(at + t, 1), :] = held[t]
-            return carry
-
-        lax.fori_loop(0, piece // step, rows, 0)
-        for start in range(0, padded, LANES):
-            block = rows_ref[start : start + LANES, :].T
-            out_ref[i, :, start : start + LANES] = block[0:vecs, :]
-        return carry
-
-    lax.fori_loop(0, panels, panel, 0)
 
 
 def exchange_start(send, out_ref, sends, recvs, me, count, place):
@@ -389,8 +354,8 @@
 
 
 def project_kernel(
-    ways, piece, total_rows, leaving_ref, basis_ref, ortho_ref, proj_ref, upper_ref,
-    landed_ref, stack_ref, near_ref, far_ref, sends, recvs, near_s, near_r, far_s, far_r,
+    ways, piece, tall, total_rows, order_ref, mine_ref, other_ref, basis_ref, ortho_ref, proj_ref, upper_ref,
+    rows_ref, table_ref, leaving_ref, landed_ref, stack_ref, near_ref, far_ref, sends, recvs, near_s, near_r, far_s, far_r,
 ):
     first, second, core, way = position()
     count = leaving_ref.shape[0]
@@ -409,7 +374,47 @@
         )
     pl.semaphore_wait(barrier, count - 1 + ways)
     group = (leaving_ref, landed_ref, sends, recvs, me, count, place)
-    exchange_start(*group)
+    padded = leaving_ref.shape[2]
+    half = tall // CORES
+    step = next(size for size in (48, 40, 32, 16, 8) if piece % size == 0)
+
+    for in_ref, which in ((mine_ref, core), (other_ref, 1 - core)):
+
+        def moment(m, carry):
+            for r in range(half):
+                start = pl.multiple_of((m * tall + half * which + r) * LANES, LANES)
+                block = jnp.concatenate([in_ref[v, m, r : r + 1, :] for v in range(vecs)], 0)
+                table_ref[pl.ds(start, LANES), 0:vecs] = block.T
+            return carry
+
+        lax.fori_loop(0, 5, moment, 0)
+
+    if padded > piece:
+        rows_ref[piece:padded, :] = jnp.zeros((padded - piece, LANES), jnp.float32)
+
+    def collect(i):
+        base = (CORES * i + core) * piece
+
+        def rows(j, carry):
+            at = pl.multiple_of(j * step, 8)
+            held = [table_ref[pl.ds(order_ref[0, base + at + t], 1), :] for t in range(step)]
+            for t in range(step):
+                rows_ref[pl.ds(at + t, 1), :] = held[t]
+            return carry
+
+        lax.fori_loop(0, piece // step, rows, 0)
+        for start in range(0, padded, LANES):
+            block = rows_ref[start : start + LANES, :].T
+            leaving_ref[i, :, start : start + LANES] = block[0:vecs, :]
+
+    def panel(d, carry):
+        to = lax.rem(me + d, count)
+        collect(to)
+        remote(leaving_ref.at[to], landed_ref.at[me], sends.at[to], recvs.at[me], place(to)).start()
+        return carry
+
+    lax.fori_loop(1, count, panel, 0)
+    collect(me)
     landed_ref[me] = leaving_ref[me]
     stack_ref[0:KB] = basis_ref[...]
     exchange_wait(*group)
@@ -539,11 +544,10 @@
     base = base.transpose(1, 0, 2, 3)
     ring = jnp.concatenate([base[:, :, tall - 2 :], base, base[:, :, : wide]], 2)
     ring = lax.dynamic_slice_in_dim(ring, core * (tall // CORES), wide, 2)
-    ring = lax.all_gather(ring, "bxy", axis=0, tiled=True)
-    part = me_first // vecs
-    if parts > 1:
-        ring = jnp.concatenate([ring, ring[:, :, :8]], 2)
-        ring = lax.dynamic_slice_in_dim(ring, part * high, piece_wide, 2)
+    rings = [ring] + [
+        lax.ppermute(ring, "bxy", [(i, (i + d) % count_first) for i in range(count_first)])
+        for d in range(1, count_first)
+    ]
 
     outgoing = basis[KB - BLK :].reshape(ways, vecs, count_first, piece).transpose(2, 0, 1, 3)
     outgoing = jnp.pad(outgoing, ((0, 0), (0, 0), (0, 0), (0, padded - piece)))
@@ -570,7 +574,12 @@
         compiler_params=params(),
         cost_estimate=cost(28),
     )(order, arrived)
+    held = lax.optimization_barrier((mine, other, *rings))
+    mine, other = held[:2]
+    ring = jnp.concatenate(held[2:], 0)
+    part = me_first // vecs
     if parts > 1:
+        ring = lax.dynamic_slice_in_dim(ring, part * high, piece_wide, 2)
         mine, other = [
             jnp.concatenate([array[:, :, s * high : s * high + piece_wide] for s in range(parts)], 0)
             for array in (mine, other)
@@ -613,28 +622,19 @@
             .reshape(vecs, 5, parts * high, third)
             for array in (back, back_other)
         ]
-    leaving = pl.pallas_call(
-        functools.partial(collect_kernel, piece, tall),
-        out_shape=jax.ShapeDtypeStruct((panels, vecs, padded), jnp.float32),
-        in_specs=[smem(), vmem(), vmem()],
-        out_specs=vmem(),
-        scratch_shapes=[
-            pltpu.VMEM((padded, LANES), jnp.float32),
-            pltpu.VMEM((slab_rows, LANES), jnp.float32),
-        ],
-        compiler_params=params(),
-        cost_estimate=cost(28),
-    )(order, back, back_other)
     return pl.pallas_call(
-        functools.partial(project_kernel, ways, piece, total_rows),
+        functools.partial(project_kernel, ways, piece, tall, total_rows),
         out_shape=(
             jax.ShapeDtypeStruct((BLK, panel_rows), jnp.float32),
             jax.ShapeDtypeStruct((KB, BLK), jnp.float32),
             jax.ShapeDtypeStruct((BLK, BLK), jnp.float32),
         ),
-        in_specs=[vmem(), vmem()],
+        in_specs=[smem(), vmem(), vmem(), vmem()],
         out_specs=(vmem(), vmem(), vmem()),
         scratch_shapes=[
+            pltpu.VMEM((padded, LANES), jnp.float32),
+            pltpu.VMEM((slab_rows, LANES), jnp.float32),
+            pltpu.VMEM((panels, vecs, padded), jnp.float32),
             pltpu.VMEM((panels, vecs, padded), jnp.float32),
             pltpu.VMEM((KB + BLK, panel_rows), jnp.float32),
             pltpu.VMEM((count_second, 32, LANES), jnp.float32),
@@ -644,8 +644,8 @@
         + semaphores(count_second, 1)
         + semaphores(count_first, 1),
         compiler_params=params(3),
-        cost_estimate=cost(20),
-    )(leaving, basis)
+        cost_estimate=cost(50),
+    )(order, back, back_other, basis)
 
 
 def solution(mesh):

time: 198 us -> 164 us (0.83)
  blocking collectives: 36.7 us -> 0 us
  starting transfers between devices: 0 us -> 12.4 us
  Pallas kernels: 153 us -> 142 us
    all_gather x1 -> x0, blocking collectives: 36.7 us -> none  [body(): ring = lax.all_gather(ring, 'bxy', axis=0, tiled=True)]
    pallas_call x2 -> x1, Pallas kernels: 62.8 us -> 50.3 us  [body(): pl.pallas_call(functools.partial(project_kernel, ways, piece, tall, total...]
    ppermute x0 -> x7, starting transfers between devices: none -> 12.4 us  [body(): lax.ppermute(ring, 'bxy', [(i, (i + d) % count_first) for i in range(coun...]
    pallas_call x1, Pallas kernels: 15.8 us -> 19.5 us  [body(): pl.pallas_call(scatter_kernel, out_shape=(half_shape, half_shape), in_spe...]
    pallas_call x1, Pallas kernels: 30.5 us -> 27.3 us  [body(): pl.pallas_call(functools.partial(spread_kernel, piece, tall), out_shape=(...]
    unnamed x8 -> x11, local copies, waits for them, and re-layouts: 3.15 us -> 4.04 us
  transfers between devices with their start and end apart: 0 -> 7, of which waited for: 0 -> 0; matrix products, arithmetic and copies ran while one was open for 0% -> 1% of each run, Pallas kernels for 0% -> 28%
where the time goes in v3:
time: 164 us
  Pallas kernels  142 us (87%)
  starting transfers between devices  12.4 us (8%)
  local copies, waits for them, and re-layouts  6.88 us (4%)
  other arithmetic  1.83 us (1%)
    pallas_call x1, Pallas kernels, body(): pl.pallas_call(functools.partial(project_kernel, ways, piece, tall, total...  50.3 us
    pallas_call x1, Pallas kernels, body(): pl.pallas_call(functools.partial(spread_kernel, piece, tall), out_shape=(...  27.3 us
    pallas_call x1, Pallas kernels, body(): pl.pallas_call(gather_kernel, out_shape=jax.ShapeDtypeStruct(block, jnp.f...  20.1 us
    pallas_call x1, Pallas kernels, body(): pl.pallas_call(scatter_kernel, out_shape=(half_shape, half_shape), in_spe...  19.5 us
    pallas_call x1, Pallas kernels, body(): pl.pallas_call(functools.partial(panels_kernel, ways), out_shape=jax.Shap...  18.4 us
    ppermute x7, starting transfers between devices, body(): lax.ppermute(ring, 'bxy', [(i, (i + d) % count_first) for i in range(coun...  12.4 us
    pallas_call x1, Pallas kernels, body(): pl.pallas_call(functools.partial(lattice_kernel, count_first, high), out_...  6.22 us
    unnamed x11, local copies, waits for them, and re-layouts  4.04 us
  transfers between devices with their start and end apart: 7, of which 0 were waited for; matrix products, arithmetic and copies ran while one was open for 1% of the time, Pallas kernels for 28%

profile of v3, /device:TPU:0, one launch (start us, length us, event | category | flops | bytes accessed | tf_op | source)
XLA Modules:
  0.0 163.8 jit_solution(17841315946100165406)
XLA Ops:
  0.6 0.0 slice-start
  0.7 0.9 convert_bitcast_fusion
  1.5 0.9 maximum_bitcast_fusion
  2.5 6.0 %collective-permute-start.6 = (f32[1,5,32,128]{3,2,1,0:T(8,128)S(1)}, f32[1,5,32,128]{3,2,1,0:T(8,128)S(1)}, u32[]{:S(2)}, u32[]{:S(2)}) collective-permute-start(f32[1,5,32,128]{3,2,1,0:T(8,128)S(1)} %fusion.1), channel_id=1, source_target_pairs={{0,28},{4,0},{8,4},{12,8},{16,12},{20,16},{24,20},{28,24},{1,29},{... | collective-permute-start | bytes 245768 | tf_op jit(solution)/shard_map/ppermute | solution.py:548
  8.6 0.4 collective-permute-start.5
  9.0 0.0 collective-permute-start.4
  9.0 3.0 %collective-permute-start.3 = (f32[1,5,32,128]{3,2,1,0:T(8,128)S(1)}, f32[1,5,32,128]{3,2,1,0:T(8,128)S(1)}, u32[]{:S(2)}, u32[]{:S(2)}) collective-permute-start(f32[1,5,32,128]{3,2,1,0:T(8,128)S(1)} %fusion.1), channel_id=1, source_target_pairs={{0,16},{4,20},{8,24},{12,28},{16,0},{20,4},{24,8},{28,12},{1,17},{... | collective-permute-start | bytes 245768 | tf_op jit(solution)/shard_map/ppermute | solution.py:548
  12.0 0.0 collective-permute-start.2
  12.0 0.0 collective-permute-done.6
  12.0 1.8 %collective-permute-start.1 = (f32[1,5,32,128]{3,2,1,0:T(8,128)S(1)}, f32[1,5,32,128]{3,2,1,0:T(8,128)S(1)}, u32[]{:S(2)}, u32[]{:S(2)}) collective-permute-start(f32[1,5,32,128]{3,2,1,0:T(8,128)S(1)} %fusion.1), channel_id=1, source_target_pairs={{0,8},{4,12},{8,16},{12,20},{16,24},{20,28},{24,0},{28,4},{1,9},{5... | collective-permute-start | bytes 245768 | tf_op jit(solution)/shard_map/ppermute | solution.py:548
  13.9 0.0 collective-permute-done.5
  13.9 1.1 collective-permute-start
  15.0 0.0 slice-done
  15.0 0.3 reshape.12
  15.3 0.3 copy.12
  15.6 0.8 pad.4
  16.4 18.4 %shard_map.76.arrived_ref = f32[16,8,1024]{2,1,0:T(8,128)} custom-call(f32[16,8,1024]{2,1,0:T(8,128)} %bitcast.11), custom_call_target="tpu_custom_call" | custom-call | bytes 43200000 | tf_op jit(solution)/shard_map/pallas_call | solution.py:555
  34.8 27.3 %shard_map.77 = (f32[8,5,32,128]{3,2,1,0:T(8,128)}, f32[8,5,32,128]{3,2,1,0:T(8,128)}) custom-call(s32[1,30720]{1,0:T(1,128)} %order_ref.3, f32[16,8,1024]{2,1,0:T(8,128)} %shard_map.76.arrived_ref), custom_call_target="tpu_custom_call" | custom-call | bytes 100800000 | tf_op jit(solution)/shard_map/pallas_call | solution.py:565
  62.1 0.0 collective-permute-done.4
  62.1 0.0 collective-permute-done.3
  62.1 0.0 collective-permute-done.2
  62.1 0.0 collective-permute-done.1
  62.1 0.0 collective-permute-done
  62.1 20.1 %shard_map.78.fields_ref = f32[8,5,32,128]{3,2,1,0:T(8,128)} custom-call(f32[8,5,32,128]{3,2,1,0:T(8,128)} %get-tuple-element.19.mine_ref, f32[8,5,32,128]{3,2,1,0:T(8,128)} %get-tuple-element.20.other_ref), custom_call_target="tpu_custom_call" | custom-call | bytes 43200000 | tf_op jit(solution)/shard_map/pallas_call | solution.py:588
  82.4 0.0 copy-start
  82.4 0.8 copy-done
  83.3 6.2 %shard_map.79.evolved_ref = f32[8,5,24,128]{3,2,1,0:T(8,128)} custom-call(f32[8,5,32,128]{3,2,1,0:T(8,128)} %shard_map.78.fields_ref, f32[8,5,32,128]{3,2,1,0:T(8,128)} %copy-done), custom_call_target="tpu_custom_call" | custom-call | tf_op jit(solution)/shard_map/pallas_call | solution.py:599
  89.5 19.5 %shard_map.80 = (f32[8,5,24,128]{3,2,1,0:T(8,128)}, f32[8,5,24,128]{3,2,1,0:T(8,128)}) custom-call(f32[8,5,24,128]{3,2,1,0:T(8,128)} %shard_map.79.evolved_ref), custom_call_target="tpu_custom_call" | custom-call | bytes 43200000 | tf_op jit(solution)/shard_map/pallas_call | solution.py:609
  109.0 50.3 %shard_map.81 = (f32[16,7680]{1,0:T(8,128)}, f32[48,16]{1,0:T(8,128)}, f32[16,16]{1,0:T(8,128)}) custom-call(s32[1,30720]{1,0:T(1,128)} %order_ref.3, f32[8,5,24,128]{3,2,1,0:T(8,128)} %get-tuple-element.29.mine_ref, f32[8,5,24,128]{3,2,1,0:T(8,128)} %get-tuple-element.30.other_ref, f32[48,7680]{1,0:T(8,128)} %basis_ref.1), custom_call_target="tpu_custom_call" | custom-call | bytes 180000000 | tf_op jit(solution)/shard_map/pallas_call | solution.py:625
  159.2 1.4 copy.10
  160.6 1.8 %copy.22 = f32[16,7680]{1,0:T(8,128)} copy(f32[16,7680]{1,0:T(8,128)} %get-tuple-element.39) | data formatting | bytes 983040
  162.5 1.3 copy.23
  (12 shorter events, 0.1 us)
Async XLA Ops:
  0.6 14.4 %slice-start = ((f32[48,7680]{1,0:T(8,128)}), f32[16,7680]{1,0:T(8,128)S(1)}, s32[]{:S(2)}) async-start(f32[48,7680]{1,0:T(8,128)} %basis_ref.1), calls=%async_computation | async-start | bytes 983040 | tf_op jit(solution)/shard_map/slice | solution.py:552
  2.5 9.5 %collective-permute-start.6 = (f32[1,5,32,128]{3,2,1,0:T(8,128)S(1)}, f32[1,5,32,128]{3,2,1,0:T(8,128)S(1)}, u32[]{:S(2)}, u32[]{:S(2)}) collective-permute-start(f32[1,5,32,128]{3,2,1,0:T(8,128)S(1)} %fusion.1), channel_id=1, source_target_pairs={{0,28},{4,0},{8,4},{12,8},{16,12},{20,16},{24,20},{28,24},{1,29},{... | collective-permute-start | bytes 245768 | tf_op jit(solution)/shard_map/ppermute | solution.py:548
  8.6 5.3 %collective-permute-start.5 = (f32[1,5,32,128]{3,2,1,0:T(8,128)S(1)}, f32[1,5,32,128]{3,2,1,0:T(8,128)S(1)}, u32[]{:S(2)}, u32[]{:S(2)}) collective-permute-start(f32[1,5,32,128]{3,2,1,0:T(8,128)S(1)} %fusion.1), channel_id=1, source_target_pairs={{0,24},{4,28},{8,0},{12,4},{16,8},{20,12},{24,16},{28,20},{1,25},{... | collective-permute-start | bytes 245768 | tf_op jit(solution)/shard_map/ppermute | solution.py:548
  9.0 53.1 %collective-permute-start.4 = (f32[1,5,32,128]{3,2,1,0:T(8,128)S(1)}, f32[1,5,32,128]{3,2,1,0:T(8,128)S(1)}, u32[]{:S(2)}, u32[]{:S(2)}) collective-permute-start(f32[1,5,32,128]{3,2,1,0:T(8,128)S(1)} %fusion.1), channel_id=1, source_target_pairs={{0,20},{4,24},{8,28},{12,0},{16,4},{20,8},{24,12},{28,16},{1,21},{... | collective-permute-start | bytes 245768 | tf_op jit(solution)/shard_map/ppermute | solution.py:548
  9.0 53.1 %collective-permute-start.3 = (f32[1,5,32,128]{3,2,1,0:T(8,128)S(1)}, f32[1,5,32,128]{3,2,1,0:T(8,128)S(1)}, u32[]{:S(2)}, u32[]{:S(2)}) collective-permute-start(f32[1,5,32,128]{3,2,1,0:T(8,128)S(1)} %fusion.1), channel_id=1, source_target_pairs={{0,16},{4,20},{8,24},{12,28},{16,0},{20,4},{24,8},{28,12},{1,17},{... | collective-permute-start | bytes 245768 | tf_op jit(solution)/shard_map/ppermute | solution.py:548
  12.0 50.1 %collective-permute-start.2 = (f32[1,5,32,128]{3,2,1,0:T(8,128)S(1)}, f32[1,5,32,128]{3,2,1,0:T(8,128)S(1)}, u32[]{:S(2)}, u32[]{:S(2)}) collective-permute-start(f32[1,5,32,128]{3,2,1,0:T(8,128)S(1)} %fusion.1), channel_id=1, source_target_pairs={{0,12},{4,16},{8,20},{12,24},{16,28},{20,0},{24,4},{28,8},{1,13},{... | collective-permute-start | bytes 245768 | tf_op jit(solution)/shard_map/ppermute | solution.py:548
  12.0 50.1 %collective-permute-start.1 = (f32[1,5,32,128]{3,2,1,0:T(8,128)S(1)}, f32[1,5,32,128]{3,2,1,0:T(8,128)S(1)}, u32[]{:S(2)}, u32[]{:S(2)}) collective-permute-start(f32[1,5,32,128]{3,2,1,0:T(8,128)S(1)} %fusion.1), channel_id=1, source_target_pairs={{0,8},{4,12},{8,16},{12,20},{16,24},{20,28},{24,0},{28,4},{1,9},{5... | collective-permute-start | bytes 245768 | tf_op jit(solution)/shard_map/ppermute | solution.py:548
  13.9 48.2 %collective-permute-start = (f32[1,5,32,128]{3,2,1,0:T(8,128)S(1)}, f32[1,5,32,128]{3,2,1,0:T(8,128)S(1)}, u32[]{:S(2)}, u32[]{:S(2)}) collective-permute-start(f32[1,5,32,128]{3,2,1,0:T(8,128)S(1)} %fusion.1), channel_id=1, source_target_pairs={{0,4},{4,8},{8,12},{12,16},{16,20},{20,24},{24,28},{28,0},{1,5},{5... | collective-permute-start | bytes 245768 | tf_op jit(solution)/shard_map/ppermute | solution.py:548
  82.4 0.9 copy-start

commit v4 on v3

--- a/solution.py
+++ b/solution.py
@@ -91,15 +91,14 @@
 def lattice_kernel(count, high, fields_ref, base_ref, out_ref, first_ref, second_ref):
     wide = fields_ref.shape[2]
 
-    me = lax.axis_index("bxy")
-
-    def base_at(place):
-        x = lax.rem(me + count - place, count)
-        return (
-            [base_ref[x, 0], base_ref[x, 1], base_ref[x, 2]],
-            base_ref[x, 3],
-            base_ref[x, 4] > 0.5,
-        )
+    ways = base_ref.shape[0]
+
+    def base_at(x):
+        held = [
+            base_ref[0, x, m] if ways == 1 else jnp.concatenate([base_ref[k, x, m] for k in range(ways)], 0)
+            for m in range(5)
+        ]
+        return (held[:3], held[3], held[4] > 0.5)
 
     def force(number, warmth):
         return 3.0 * FLOW_WEIGHTS[number] * FLOW_DIRS[number][1] * BUOYANCY * warmth
@@ -192,15 +191,17 @@
 
     lax.fori_loop(0, panels, panel, 0)
 
-    for out_ref, which in ((mine_ref, core), (other_ref, 1 - core)):
+    for out_ref, next_ref, which in ((mine_ref, other_ref, core), (other_ref, mine_ref, 1 - core)):
 
         def moment(m, carry):
-            for r in range(wide):
+            for r in range(half):
                 level = lax.rem(half * which + tall - 2 + r, tall)
                 start = pl.multiple_of((m * tall + level) * LANES, LANES)
                 block = spread_ref[pl.ds(start, LANES), :].T
                 for v in range(vecs):
                     out_ref[v, m, r : r + 1, :] = block[v : v + 1, :]
+                    if half + r < wide:
+                        next_ref[v, m, half + r : half + r + 1, :] = block[v : v + 1, :]
             return carry
 
         lax.fori_loop(0, 5, moment, 0)
@@ -263,21 +264,82 @@
     return (first, second, lax.rem(second, CORES), second // CORES)
 
 
-def panels_kernel(ways, outgoing_ref, arrived_ref, sends, recvs):
-    first, _, core, way = position()
-    count = outgoing_ref.shape[0]
+def panels_kernel(ways, outgoing_ref, share_ref, arrived_ref, base_ref, sends, recvs, base_s, base_r, pass_s, pass_r):
+    first, second, core, way = position()
+    count, count_first = outgoing_ref.shape[0], base_ref.shape[1]
     me = first * ways + way
 
     def place(i):
         return (i // ways, lax.rem(i, ways) * CORES + core)
+
+    def along_first(d):
+        to = lax.rem(first + d, count_first)
+        return remote(share_ref, base_ref.at[way, first], base_s.at[to], base_r.at[first], (to, second))
+
+    def landed(source):
+        return remote(
+            share_ref, base_ref.at[way, source], base_s.at[source], base_r.at[source], (source, second)
+        )
+
+    def onward(source, k):
+        to = lax.rem(way + k, ways)
+        return remote(
+            base_ref.at[way, source],
+            base_ref.at[way, source],
+            pass_s.at[to, source],
+            pass_r.at[way, source],
+            (first, to * CORES + core),
+        )
+
+    def handed(source, k):
+        giver = lax.rem(way + k, ways)
+        return remote(
+            base_ref.at[giver, source],
+            base_ref.at[giver, source],
+            pass_s.at[giver, source],
+            pass_r.at[giver, source],
+            (first, giver * CORES + core),
+        )
 
     greet(me, count, place)
     pl.semaphore_wait(pltpu.get_barrier_semaphore(), count - 1)
     group = (outgoing_ref, arrived_ref, sends, recvs, me, count, place)
+
+    def begin(d, carry):
+        along_first(d).start()
+        return carry
+
+    lax.fori_loop(1, count_first, begin, 0)
     exchange_start(*group)
     arrived_ref[me] = outgoing_ref[me]
+    base_ref[way, first] = share_ref[...]
+    for k in range(1, ways):
+        onward(first, k).start()
+
+    def relay(d, carry):
+        source = lax.rem(first + count_first - d, count_first)
+        landed(source).wait_recv()
+        for k in range(1, ways):
+            onward(source, k).start()
+        return carry
+
+    lax.fori_loop(1, count_first, relay, 0)
     exchange_wait(*group)
     exchange_drain(*group)
+
+    def drain(d, carry):
+        along_first(d).wait_send()
+        return carry
+
+    lax.fori_loop(1, count_first, drain, 0)
+
+    def end(source, carry):
+        for k in range(1, ways):
+            handed(source, k).wait_recv()
+            onward(source, k).wait_send()
+        return carry
+
+    lax.fori_loop(0, count_first, end, 0)
 
 
 def gather_kernel(mine_ref, other_ref, out_ref, got_ref, mix_ref, swap_s, swap_r, sends, recvs):
@@ -543,24 +605,27 @@
     base = jnp.concatenate([velocity, temper[None], solid.astype(jnp.float32)[None]], 0)
     base = base.transpose(1, 0, 2, 3)
     ring = jnp.concatenate([base[:, :, tall - 2 :], base, base[:, :, : wide]], 2)
-    ring = lax.dynamic_slice_in_dim(ring, core * (tall // CORES), wide, 2)
-    rings = [ring] + [
-        lax.ppermute(ring, "bxy", [(i, (i + d) % count_first) for i in range(count_first)])
-        for d in range(1, count_first)
-    ]
+    way = lax.axis_index("bz") // CORES
+    rows = wide // ways
+    ring = lax.dynamic_slice_in_dim(ring, core * (tall // CORES) + way * rows, rows, 2)[0]
 
     outgoing = basis[KB - BLK :].reshape(ways, vecs, count_first, piece).transpose(2, 0, 1, 3)
     outgoing = jnp.pad(outgoing, ((0, 0), (0, 0), (0, 0), (0, padded - piece)))
     outgoing = outgoing.reshape(panels, vecs, padded)
-    arrived = pl.pallas_call(
+    arrived, ring = pl.pallas_call(
         functools.partial(panels_kernel, ways),
-        out_shape=jax.ShapeDtypeStruct((panels, vecs, padded), jnp.float32),
-        in_specs=[vmem()],
-        out_specs=vmem(),
-        scratch_shapes=semaphores(panels, 1),
+        out_shape=(
+            jax.ShapeDtypeStruct((panels, vecs, padded), jnp.float32),
+            jax.ShapeDtypeStruct((ways, count_first, 5, rows, third), jnp.float32),
+        ),
+        in_specs=[vmem(), vmem()],
+        out_specs=(vmem(), vmem()),
+        scratch_shapes=semaphores(panels, 1)
+        + semaphores(count_first, 1)
+        + [pltpu.SemaphoreType.DMA((ways, count_first))] * 2,
         compiler_params=params(0),
-        cost_estimate=cost(12),
-    )(outgoing)
+        cost_estimate=cost(18),
+    )(outgoing, ring)
     part_shape = jax.ShapeDtypeStruct((vecs, 5, wide, third), jnp.float32)
     mine, other = pl.pallas_call(
         functools.partial(spread_kernel, piece, tall),
@@ -574,12 +639,10 @@
         compiler_params=params(),
         cost_estimate=cost(28),
     )(order, arrived)
-    held = lax.optimization_barrier((mine, other, *rings))
-    mine, other = held[:2]
-    ring = jnp.concatenate(held[2:], 0)
     part = me_first // vecs
     if parts > 1:
-        ring = lax.dynamic_slice_in_dim(ring, part * high, piece_wide, 2)
+        ring = ring.transpose(1, 2, 0, 3, 4).reshape(count_first, 5, wide, third)
+        ring = lax.dynamic_slice_in_dim(ring, part * high, piece_wide, 2)[None]
         mine, other = [
             jnp.concatenate([array[:, :, s * high : s * high + piece_wide] for s in range(parts)], 0)
             for array in (mine, other)

time: 164 us -> 158 us (0.963)
  starting transfers between devices: 12.4 us -> 0 us
  Pallas kernels: 142 us -> 148 us
    ppermute x7 -> x0, starting transfers between devices: 12.4 us -> none  [body(): lax.ppermute(ring, 'bxy', [(i, (i + d) % count_first) for i in range(coun...]
    pallas_call x1, Pallas kernels: 18.4 us -> 24.9 us  [body(): pl.pallas_call(functools.partial(panels_kernel, ways), out_shape=(jax.Sha...]
    unnamed x11 -> x2, local copies, waits for them, and re-layouts: 4.04 us -> 3.13 us
  transfers between devices with their start and end apart: 7 -> 0, of which waited for: 0 -> 0; matrix products, arithmetic and copies ran while one was open for 1% -> 0% of each run, Pallas kernels for 28% -> 0%
where the time goes in v4:
time: 158 us
  Pallas kernels  148 us (94%)
  local copies, waits for them, and re-layouts  5.97 us (4%)
  other arithmetic  2.44 us (2%)
    pallas_call x1, Pallas kernels, body(): pl.pallas_call(functools.partial(project_kernel, ways, piece, tall, total...  50.9 us
    pallas_call x1, Pallas kernels, body(): pl.pallas_call(functools.partial(spread_kernel, piece, tall), out_shape=(...  26 us
    pallas_call x1, Pallas kernels, body(): pl.pallas_call(functools.partial(panels_kernel, ways), out_shape=(jax.Sha...  24.9 us
    pallas_call x1, Pallas kernels, body(): pl.pallas_call(gather_kernel, out_shape=jax.ShapeDtypeStruct(block, jnp.f...  20.7 us
    pallas_call x1, Pallas kernels, body(): pl.pallas_call(scatter_kernel, out_shape=(half_shape, half_shape), in_spe...  19.7 us
    pallas_call x1, Pallas kernels, body(): pl.pallas_call(functools.partial(lattice_kernel, count_first, high), out_...  6.2 us

profile of v4, /device:TPU:0, one launch (start us, length us, event | category | flops | bytes accessed | tf_op | source)
XLA Modules:
  0.0 157.6 jit_solution(15037651386267567678)
XLA Ops:
  0.6 0.0 slice-start
  0.7 0.9 convert_bitcast_fusion
  1.5 0.9 maximum_bitcast_fusion
  2.5 0.6 fusion.2.share_ref
  3.1 0.0 slice-done
  3.1 0.3 reshape.12
  3.4 0.3 copy.11
  3.7 0.8 pad.4
  4.6 24.9 %shard_map.76 = (f32[16,8,1024]{2,1,0:T(8,128)}, f32[2,8,5,16,128]{4,3,2,1,0:T(8,128)}) custom-call(f32[16,8,1024]{2,1,0:T(8,128)} %bitcast.11, f32[5,16,128]{2,1,0:T(8,128)} %fusion.2.share_ref), custom_call_target="tpu_custom_call" | custom-call | bytes 64800000 | tf_op jit(solution)/shard_map/pallas_call | solution.py:615
  29.5 26.0 %shard_map.77 = (f32[8,5,32,128]{3,2,1,0:T(8,128)}, f32[8,5,32,128]{3,2,1,0:T(8,128)}) custom-call(s32[1,30720]{1,0:T(1,128)} %order_ref.3, f32[16,8,1024]{2,1,0:T(8,128)} %get-tuple-element.9.arrived_ref), custom_call_target="tpu_custom_call" | custom-call | bytes 100800000 | tf_op jit(solution)/shard_map/pallas_call | solution.py:630
  55.5 20.7 %shard_map.78.fields_ref = f32[8,5,32,128]{3,2,1,0:T(8,128)} custom-call(f32[8,5,32,128]{3,2,1,0:T(8,128)} %get-tuple-element.10.mine_ref, f32[8,5,32,128]{3,2,1,0:T(8,128)} %get-tuple-element.11.other_ref), custom_call_target="tpu_custom_call" | custom-call | bytes 43200000 | tf_op jit(solution)/shard_map/pallas_call | solution.py:651
  76.2 6.2 %shard_map.79.evolved_ref = f32[8,5,24,128]{3,2,1,0:T(8,128)} custom-call(f32[8,5,32,128]{3,2,1,0:T(8,128)} %shard_map.78.fields_ref, f32[2,8,5,16,128]{4,3,2,1,0:T(8,128)} %get-tuple-element.12.base_ref), custom_call_target="tpu_custom_call" | custom-call | tf_op jit(solution)/shard_map/pallas_call | solution.py:662
  82.4 19.7 %shard_map.80 = (f32[8,5,24,128]{3,2,1,0:T(8,128)}, f32[8,5,24,128]{3,2,1,0:T(8,128)}) custom-call(f32[8,5,24,128]{3,2,1,0:T(8,128)} %shard_map.79.evolved_ref), custom_call_target="tpu_custom_call" | custom-call | bytes 43200000 | tf_op jit(solution)/shard_map/pallas_call | solution.py:672
  102.1 50.9 %shard_map.81 = (f32[16,7680]{1,0:T(8,128)}, f32[48,16]{1,0:T(8,128)}, f32[16,16]{1,0:T(8,128)}) custom-call(s32[1,30720]{1,0:T(1,128)} %order_ref.3, f32[8,5,24,128]{3,2,1,0:T(8,128)} %get-tuple-element.13.mine_ref, f32[8,5,24,128]{3,2,1,0:T(8,128)} %get-tuple-element.14.other_ref, f32[48,7680]{1,0:T(8,128)} %basis_ref.1), custom_call_target="tpu_custom_call" | custom-call | bytes 180000000 | tf_op jit(solution)/shard_map/pallas_call | solution.py:688
  153.0 1.4 copy.9
  154.4 1.8 %copy.14 = f32[16,7680]{1,0:T(8,128)} copy(f32[16,7680]{1,0:T(8,128)} %get-tuple-element.23) | data formatting | bytes 983040
  156.3 1.3 copy.15
  (3 shorter events, 0.0 us)
Async XLA Ops:
  0.6 2.5 %slice-start = ((f32[48,7680]{1,0:T(8,128)}), f32[16,7680]{1,0:T(8,128)S(1)}, s32[]{:S(2)}) async-start(f32[48,7680]{1,0:T(8,128)} %basis_ref.1), calls=%async_computation | async-start | bytes 983040 | tf_op jit(solution)/shard_map/slice | solution.py:612
